TPU v7x, 32 devices: a whole 2x2x4 slice. The times are simulated.
32 devices in a mesh: gx: 4 (over y, core), gy: 8 (over z, x).
Axes of the slice: x: 2, y: 2, z: 4, core: 2. Of those that a mesh axis runs over, the one named last changes fastest.
Arguments:
- patches: bfloat16 [3072, 1408], P(('gx', 'gy')), may hold values from -6 to 6
- grids: int32 [8, 2], replicated, may hold values from 4 to 12, as said below
- text_ids: int32 [2048], P('gx'), may hold values from 0 to 31999
- positions: int32 [768], replicated, may hold values from -1 to 1023, as said below
- lengths: int32 [8], replicated, may hold values from 1 to 1536, 2048 in all
- text_table: bfloat16 [32000, 1408], P('gy'), may hold values from -6 to 6
- vit_norm1: float32 [1408], replicated, may hold values from 0.5 to 1.5
- vit_qkv: bfloat16 [1408, 3, 1408], P('gx', None, 'gy'), may hold values from -0.15625 to 0.15625
- vit_out: bfloat16 [1408, 1408], P('gx', 'gy'), may hold values from -0.15625 to 0.15625
- vit_norm2: float32 [1408], replicated, may hold values from 0.5 to 1.5
- vit_fc1: bfloat16 [1408, 6144], P('gx', 'gy'), may hold values from -0.15625 to 0.15625
- vit_fc2: bfloat16 [1408, 6144], P('gx', 'gy'), may hold values from -0.078125 to 0.078125
- merge_norm: float32 [4, 1408], replicated, may hold values from 0.5 to 1.5
- merge_proj: bfloat16 [1408, 4, 1408], P('gx', None, 'gy'), may hold values from -0.078125 to 0.078125
- dec_norm1: float32 [1408], replicated, may hold values from 0.5 to 1.5
- dec_qkv: bfloat16 [1408, 3, 1408], P('gx', None, 'gy'), may hold values from -0.15625 to 0.15625
- dec_out: bfloat16 [1408, 1408], P('gx', 'gy'), may hold values from -0.15625 to 0.15625
- dec_norm2: float32 [1408], replicated, may hold values from 0.5 to 1.5
- dec_fc1: bfloat16 [1408, 6144], P('gx', 'gy'), may hold values from -0.15625 to 0.15625
- dec_fc2: bfloat16 [1408, 6144], P('gx', 'gy'), may hold values from -0.078125 to 0.078125
- next_norm: float32 [1408], replicated, may hold values from 0.5 to 1.5
- next_qkv: bfloat16 [1408, 3, 1408], P('gx', None, 'gy'), may hold values from -0.15625 to 0.15625
Outputs:
- next_triple: bfloat16 [2048, 3, 1408], P(('gx', 'gy'))
Inputs may be any that keep to these rules, and one draw needn't show every extreme that they name: `grids`: row i gives image i's merged grid (rows from (9) // 2 to 8, columns from (13) // 2 to 12); images i * 2 to i * 2 + 1 belong to index i of gx; in every draw all images of some index of gx have 8 x 12, filling its 768 patch slots. Each index of gx's merged slots that belong to images come first; they hold distinct prompt positions that rise with the slot's global index; the other slots hold -1.
All inputs are finite; a program needn't handle non-finite values.
Results may differ from a plain program's by a relative error of at most 0.023.
Values may be sent and summed in bfloat16 or wider, within the bound.
A program may use at most 128 MiB of HBM per device.

v0:
```python
import jax
import jax.numpy as jnp
from jax import lax
from jax.sharding import PartitionSpec as P

HEAD_DIM = 88


norm_eps = 1e-06


def layer_norm(values, gain_row):
    values = values.astype(jnp.float32)
    centre = values - jnp.mean(values, axis=-1, keepdims=True)
    spread = jnp.mean(centre * centre, axis=-1, keepdims=True)
    return (centre * lax.rsqrt(spread + norm_eps) * gain_row).astype(jnp.bfloat16)


def rms_norm(values, gain_row):
    values = values.astype(jnp.float32)
    square = jnp.mean(values * values, axis=-1, keepdims=True)
    return (values * lax.rsqrt(square + norm_eps) * gain_row).astype(jnp.bfloat16)


def image_bounds(grid_rows):
    merged_count = grid_rows[:, 0] * grid_rows[:, 1]
    merged_end = jnp.cumsum(merged_count)
    return (merged_count, merged_end)


def patch_images(grid_rows, patch_slots):
    merged_count, merged_end = image_bounds(grid_rows)
    slot_index = jnp.arange(patch_slots, dtype=jnp.int32)
    return jnp.sum((slot_index[:, None] >= 4 * merged_end[None, :]).astype(jnp.int32), axis=1)


def merge_sources(grid_rows, merge_slots):
    image_count = grid_rows.shape[0]
    merged_count, merged_end = image_bounds(grid_rows)
    merged_start = merged_end - merged_count
    slot_index = jnp.arange(merge_slots, dtype=jnp.int32)
    image_of = jnp.sum((slot_index[:, None] >= merged_end[None, :]).astype(jnp.int32), axis=1)
    is_live = image_of < image_count
    picked = (
        jnp.minimum(image_of, image_count - 1)[:, None]
        == jnp.arange(image_count, dtype=jnp.int32)[None, :]
    ).astype(jnp.int32)
    col_count = jnp.sum(picked * grid_rows[None, :, 1], axis=1)
    first_slot = jnp.sum(picked * merged_start[None, :], axis=1)
    local_slot = slot_index - first_slot
    grid_row = local_slot // col_count
    grid_col = local_slot % col_count
    base_row = 4 * first_slot + 4 * grid_row * col_count + 2 * grid_col
    offsets = jnp.stack(
        [jnp.zeros_like(col_count), jnp.ones_like(col_count), 2 * col_count, 2 * col_count + 1],
        axis=1,
    )
    return jnp.where(is_live[:, None], base_row[:, None] + offsets, 0)


def request_of(index_rows, bounds):
    return jnp.sum((index_rows[:, None] >= bounds[None, :]).astype(jnp.int32), axis=1)


def local_heads(queries, key_rows, value_rows, allowed):
    scores = jnp.einsum(
        "qhe,khe->hqk", queries, key_rows, preferred_element_type=jnp.float32
    ) * HEAD_DIM ** (-0.5)
    exp_scores = jnp.where(allowed[None], jnp.exp(scores), 0.0)
    denominator = jnp.sum(exp_scores, axis=2)
    weighted = jnp.einsum(
        "hqk,khe->qhe",
        exp_scores.astype(jnp.bfloat16),
        value_rows,
        preferred_element_type=jnp.float32,
    )
    result = (weighted / denominator.T[:, :, None]).astype(jnp.bfloat16)
    return result.reshape(queries.shape[0], -1)


def spread_features(values):
    return lax.all_gather(values, "gy", axis=1, tiled=True)


def fold_rows(blocks, step_fn, initial):
    return step_fn(initial, lax.all_gather(blocks, "gx", axis=0, tiled=True), jnp.int32(0))


def dense(left_rows, weight):
    trailing = weight.shape[1:]
    flat_width = 1
    for extent in trailing:
        flat_width = flat_width * extent
    initial = jnp.zeros((left_rows.shape[0], flat_width), jnp.float32)

    def accumulate(running, block_rows, offset):
        return jnp.dot(
            left_rows,
            block_rows.reshape(block_rows.shape[0], flat_width),
            preferred_element_type=jnp.float32,
        )

    return fold_rows(weight, accumulate, initial).reshape((left_rows.shape[0],) + trailing)


def down_columns(hidden, weight):
    return lax.dot_general(
        hidden,
        lax.all_gather(weight, "gx", axis=0, tiled=True),
        (((1,), (1,)), ((), ())),
        preferred_element_type=jnp.float32,
    )


def feed_forward(stream_full, gain_row, fc_in, fc_back, norm_fn):
    hidden = jax.nn.gelu(dense(norm_fn(stream_full, gain_row), fc_in), approximate=False).astype(
        jnp.bfloat16
    )
    partial_sum = down_columns(hidden, fc_back)
    summed = lax.psum(partial_sum.astype(jnp.bfloat16), "gy").astype(jnp.float32)
    return (stream_full.astype(jnp.float32) + summed).astype(jnp.bfloat16)


def per_device(
    patches,
    grids,
    text_ids,
    positions,
    lengths,
    text_table,
    vit_norm1,
    vit_qkv,
    vit_out,
    vit_norm2,
    vit_fc1,
    vit_fc2,
    merge_norm,
    merge_proj,
    dec_norm1,
    dec_qkv,
    dec_out,
    dec_norm2,
    dec_fc1,
    dec_fc2,
    next_norm,
    next_qkv,
):
    gx_count = lax.axis_size("gx")
    gx_index = lax.axis_index("gx")
    gy_index = lax.axis_index("gy")
    per_group = grids.shape[0] // gx_count
    own_grids = lax.dynamic_slice_in_dim(grids, gx_index * per_group, per_group, 0)
    local_width = vit_qkv.shape[2]
    head_count = local_width // HEAD_DIM
    patches_full = lax.all_gather(patches, "gy", axis=0, tiled=True)
    patch_slots = patches_full.shape[0]
    patches_local = lax.dynamic_slice_in_dim(patches_full, gy_index * local_width, local_width, 1)
    triple = dense(layer_norm(patches_full, vit_norm1), vit_qkv).astype(jnp.bfloat16)
    triple = triple.reshape(patch_slots, 3, head_count, HEAD_DIM)
    image_ids = patch_images(own_grids, patch_slots)
    attended = local_heads(
        triple[:, 0], triple[:, 1], triple[:, 2], image_ids[:, None] == image_ids[None, :]
    )
    vit_mid = (
        patches_local.astype(jnp.float32) + dense(spread_features(attended), vit_out)
    ).astype(jnp.bfloat16)
    vit_final = feed_forward(spread_features(vit_mid), vit_norm2, vit_fc1, vit_fc2, layer_norm)
    full_width = vit_final.shape[1]
    merge_slots = positions.shape[0] // gx_count
    sources = merge_sources(own_grids, merge_slots).reshape(merge_slots * 4)
    merged = jnp.take(vit_final, sources, axis=0).reshape(merge_slots, 4 * full_width)
    merged_normed = layer_norm(merged, merge_norm.reshape(-1)).reshape(merge_slots, 4, full_width)

    def add_merged(running, block_rows, offset):
        return jnp.einsum(
            "mkd,dko->mo", merged_normed, block_rows, preferred_element_type=jnp.float32
        )

    projected = fold_rows(
        merge_proj, add_merged, jnp.zeros((merge_slots, local_width), jnp.float32)
    ).astype(jnp.bfloat16)
    seq_slots = text_ids.shape[0]
    seq_index = gx_index * seq_slots + jnp.arange(seq_slots, dtype=jnp.int32)

    def place_rows(running, block_rows, offset):
        chosen = (positions[None, :] == seq_index[:, None]).astype(jnp.bfloat16)
        return jnp.dot(chosen, block_rows, preferred_element_type=jnp.float32)

    placed = fold_rows(projected, place_rows, jnp.zeros((seq_slots, local_width), jnp.float32))
    is_image = jnp.any(positions[None, :] == seq_index[:, None], axis=1)
    vocab_rows = text_table.shape[0]
    shifted_ids = text_ids - gy_index * vocab_rows
    inside = (shifted_ids >= 0) & (shifted_ids < vocab_rows)
    looked_up = jnp.take(text_table, jnp.clip(shifted_ids, 0, vocab_rows - 1), axis=0)
    table_terms = jnp.where(inside[:, None], looked_up.astype(jnp.float32), 0.0)
    text_rows = lax.psum_scatter(
        table_terms.astype(jnp.bfloat16), "gy", scatter_dimension=1, tiled=True
    )
    embedded = jnp.where(is_image[:, None], placed.astype(jnp.bfloat16), text_rows)
    dec_triple = dense(rms_norm(spread_features(embedded), dec_norm1), dec_qkv).astype(jnp.bfloat16)
    queries = dec_triple[:, 0].reshape(seq_slots, head_count, HEAD_DIM)
    bounds = jnp.cumsum(lengths)
    own_request = request_of(seq_index, bounds)
    key_rows = lax.all_gather(dec_triple[:, 1], "gx", axis=0, tiled=True)
    value_rows = lax.all_gather(dec_triple[:, 2], "gx", axis=0, tiled=True)
    key_count = key_rows.shape[0]
    key_index = jnp.arange(key_count, dtype=jnp.int32)
    allowed = (request_of(key_index, bounds)[None, :] == own_request[:, None]) & (
        key_index[None, :] <= seq_index[:, None]
    )
    scores = jnp.einsum(
        "qhe,khe->hqk",
        queries,
        key_rows.reshape(key_count, head_count, HEAD_DIM),
        preferred_element_type=jnp.float32,
    ) * HEAD_DIM ** (-0.5)
    exp_scores = jnp.where(allowed[None], jnp.exp(scores), 0.0)
    denominator = jnp.sum(exp_scores, axis=2)
    weighted = jnp.einsum(
        "hqk,khe->hqe",
        exp_scores.astype(jnp.bfloat16),
        value_rows.reshape(key_count, head_count, HEAD_DIM),
        preferred_element_type=jnp.float32,
    )
    denominator, weighted = (denominator, weighted)
    dec_attended = (
        (weighted / denominator[:, :, None])
        .astype(jnp.bfloat16)
        .transpose(1, 0, 2)
        .reshape(seq_slots, local_width)
    )
    dec_mid = (embedded.astype(jnp.float32) + dense(spread_features(dec_attended), dec_out)).astype(
        jnp.bfloat16
    )
    dec_final = feed_forward(spread_features(dec_mid), dec_norm2, dec_fc1, dec_fc2, rms_norm)
    next_local = dense(rms_norm(dec_final, next_norm), next_qkv).astype(jnp.bfloat16)
    return lax.all_to_all(next_local, "gy", split_axis=0, concat_axis=2, tiled=True)


def solution(mesh):
    placed = (
        P(("gx", "gy"), None),
        P(),
        P("gx"),
        P(),
        P(),
        P("gy", None),
        P(),
        P("gx", None, "gy"),
        P("gx", "gy"),
        P(),
        P("gx", "gy"),
        P("gx", "gy"),
        P(),
        P("gx", None, "gy"),
        P(),
        P("gx", None, "gy"),
        P("gx", "gy"),
        P(),
        P("gx", "gy"),
        P("gx", "gy"),
        P(),
        P("gx", None, "gy"),
    )
    return jax.shard_map(
        per_device,
        mesh=mesh,
        in_specs=placed,
        out_specs=P(("gx", "gy"), None, None),
        check_vma=False,
    )
```

profile of v0, /device:TPU:8, one launch (start us, length us, event | category | flops | bytes accessed | tf_op | source)
XLA Modules:
  0.0 848.1 jit_solution(16821582663121444861)
XLA Ops:
  10.3 26.9 %all-gather.22.cloned.1.call-done = bf16[1408,3,176]{2,1,0:T(4,128)(2,1)} async-done(((bf16[352,3,176]{2,1,0:T(4,128)(2,1)}), bf16[1408,3,176]{2,1,0:T(4,128)(2,1)}) %all-gather.22.cloned.1.call-update) | async-done | bytes 1486864 | tf_op jit(solution)/shard_map/all_gather | solution.py:86
  37.2 5.4 copy.118
  42.6 46.8 %all-gather.20.cloned.1.call-done = bf16[768,1408]{1,0:T(8,128)(2,1)} async-done(((bf16[96,1408]{1,0:T(8,128)(2,1)}), bf16[768,1408]{1,0:T(8,128)(2,1)}) %all-gather.20.cloned.1.call-update) | async-done | bytes 2162704 | tf_op jit(solution)/shard_map/all_gather | solution.py:155
  97.4 7.2 all-gather.2
  105.6 40.4 %all-gather.24.cloned.1.call-done = bf16[768,1408]{0,1:T(8,128)(2,1)} async-done(((bf16[768,176]{0,1:T(8,128)(2,1)}), bf16[768,1408]{0,1:T(8,128)(2,1)}) %all-gather.24.cloned.1.call-update) | async-done | bytes 2162704 | tf_op jit(solution)/shard_map/all_gather | solution.py:82
  150.6 46.9 %all-gather.26.cloned.1.call-done = bf16[768,1408]{0,1:T(8,128)(2,1)} async-done(((bf16[768,176]{0,1:T(8,128)(2,1)}), bf16[768,1408]{0,1:T(8,128)(2,1)}) %all-gather.26.cloned.1.call-update) | async-done | bytes 2162704 | tf_op jit(solution)/shard_map/all_gather | solution.py:82
  200.4 20.0 %all-gather.28.cloned.1.call-done = bf16[1408,768]{1,0:T(8,128)(2,1)} async-done(((bf16[352,768]{1,0:T(8,128)(2,1)}), bf16[1408,768]{1,0:T(8,128)(2,1)}) %all-gather.28.cloned.1.call-update) | async-done | bytes 2162704 | tf_op jit(solution)/shard_map/all_gather | solution.py:86
  220.4 24.4 %all-gather.30.cloned.1.call-done = bf16[1408,768]{1,0:T(8,128)(2,1)} async-done(((bf16[352,768]{1,0:T(8,128)(2,1)}), bf16[1408,768]{1,0:T(8,128)(2,1)}) %all-gather.30.cloned.1.call-update) | async-done | bytes 2162704 | tf_op jit(solution)/shard_map/all_gather | solution.py:109
  244.8 11.9 %convolution_convert_fusion = bf16[768,1408]{0,1:T(8,128)(2,1)} fusion(bf16[1408,768]{1,0:T(8,128)(2,1)} %all-gather.30.cloned.1.call-done, bf16[1408,768]{1,0:T(8,128)(2,1)} %all-gather.28.cloned.1.call-done, bf16[768,1408]{0,1:T(8,128)(2,1)S(1)} %copy-done.3, f32[1408]{0:T(1024)S(1)} %copy-done.18, f32[768]{0:T(1024)S(1)} %add_rsqrt_fusion, ...), kind=kOutput, calls=%fused_computation.41 | convolution fusion | flops 3366715392 | bytes 8662528 | tf_op jit(solution)/shard_map/dot_general | solution.py:107
  259.5 10.2 %gather_fusion.1 = bf16[512,1408]{1,0:T(8,128)(2,1)} fusion(bf16[4000,1408]{1,0:T(8,128)(2,1)} %param.27, s32[1024]{0:T(1024)S(1)} %pad_clamp_fusion), kind=kCustom, calls=%fused_computation.1 | custom fusion | bytes 2885632 | tf_op jit(solution)/shard_map/jit(_take)/gather | solution.py:194
  277.9 82.0 %all-reduce.3.cloned.1.call-done = bf16[768,1408]{0,1:T(8,128)(2,1)} async-done(((bf16[768,1408]{0,1:T(8,128)(2,1)}), bf16[768,1408]{0,1:T(8,128)(2,1)}) %all-reduce.3.cloned.1.call-update) | async-done | bytes 2162704 | tf_op jit(solution)/shard_map/psum | solution.py:120
  366.3 3.8 gather_fusion
  370.1 4.1 gather.11
  376.4 11.9 %all-gather.32.cloned.1.call-done = bf16[1408,4,176]{2,1,0:T(4,128)(2,1)} async-done(((bf16[352,4,176]{2,1,0:T(4,128)(2,1)}), bf16[1408,4,176]{2,1,0:T(4,128)(2,1)}) %all-gather.32.cloned.1.call-update) | async-done | bytes 1982480 | tf_op jit(solution)/shard_map/all_gather | solution.py:86
  388.3 4.2 fusion.161
  392.5 6.3 all-gather.3
  399.3 56.9 %reduce-scatter.2.cloned.1.call-done = bf16[512,176]{0,1:T(8,128)(2,1)} async-done(((bf16[512,1408]{0,1:T(8,128)(2,1)}), bf16[512,176]{0,1:T(8,128)(2,1)}) %reduce-scatter.2.cloned.1.call-update) | async-done | bytes 180240 | tf_op jit(solution)/shard_map/reduce_scatter | solution.py:196
  460.2 23.8 %all-gather.36.cloned.1.call-done = bf16[1408,3,176]{2,1,0:T(4,128)(2,1)} async-done(((bf16[352,3,176]{2,1,0:T(4,128)(2,1)}), bf16[1408,3,176]{2,1,0:T(4,128)(2,1)}) %all-gather.36.cloned.1.call-update) | async-done | bytes 1486864 | tf_op jit(solution)/shard_map/all_gather | solution.py:86
  484.0 4.3 copy.131
  488.3 40.9 %all-gather.34.cloned.1.call-done = bf16[512,1408]{0,1:T(8,128)(2,1)} async-done(((bf16[512,176]{0,1:T(8,128)(2,1)}), bf16[512,1408]{0,1:T(8,128)(2,1)}) %all-gather.34.cloned.1.call-update) | async-done | bytes 1441808 | tf_op jit(solution)/shard_map/all_gather | solution.py:82
  533.5 8.2 all-gather
  541.7 8.3 all-gather.1
  555.5 7.4 all-gather.4
  563.5 32.8 %all-gather.38.cloned.1.call-done = bf16[512,1408]{0,1:T(8,128)(2,1)} async-done(((bf16[512,176]{0,1:T(8,128)(2,1)}), bf16[512,1408]{0,1:T(8,128)(2,1)}) %all-gather.38.cloned.1.call-update) | async-done | bytes 1441808 | tf_op jit(solution)/shard_map/all_gather | solution.py:82
  601.6 38.7 %all-gather.40.cloned.1.call-done = bf16[512,1408]{0,1:T(8,128)(2,1)} async-done(((bf16[512,176]{0,1:T(8,128)(2,1)}), bf16[512,1408]{0,1:T(8,128)(2,1)}) %all-gather.40.cloned.1.call-update) | async-done | bytes 1441808 | tf_op jit(solution)/shard_map/all_gather | solution.py:82
  642.0 21.1 %all-gather.42.cloned.1.call-done = bf16[1408,768]{1,0:T(8,128)(2,1)} async-done(((bf16[352,768]{1,0:T(8,128)(2,1)}), bf16[1408,768]{1,0:T(8,128)(2,1)}) %all-gather.42.cloned.1.call-update) | async-done | bytes 2162704 | tf_op jit(solution)/shard_map/all_gather | solution.py:86
  663.1 24.4 %all-gather.44.cloned.1.call-done = bf16[1408,768]{1,0:T(8,128)(2,1)} async-done(((bf16[352,768]{1,0:T(8,128)(2,1)}), bf16[1408,768]{1,0:T(8,128)(2,1)}) %all-gather.44.cloned.1.call-update) | async-done | bytes 2162704 | tf_op jit(solution)/shard_map/all_gather | solution.py:109
  687.5 9.4 %convolution_convert_fusion.1 = bf16[512,1408]{0,1:T(8,128)(2,1)} fusion(bf16[1408,768]{1,0:T(8,128)(2,1)} %all-gather.44.cloned.1.call-done, bf16[1408,768]{1,0:T(8,128)(2,1)} %all-gather.42.cloned.1.call-done, bf16[512,1408]{0,1:T(8,128)(2,1)} %all-gather.40.cloned.1.call-done, f32[1408]{0:T(1024)S(1)} %copy-done.20, f32[512]{0:T(512)S(1)} %add_rsqrt_fusion.3), kind=kOutput, calls=%fused_computation.42 | convolution fusion | flops 2243756032 | bytes 7216640 | tf_op jit(solution)/shard_map/dot_general | solution.py:107
  696.9 19.1 %all-gather.46.cloned.1.call-done = bf16[1408,3,176]{2,1,0:T(4,128)(2,1)} async-done(((bf16[352,3,176]{2,1,0:T(4,128)(2,1)}), bf16[1408,3,176]{2,1,0:T(4,128)(2,1)}) %all-gather.46.cloned.1.call-update) | async-done | bytes 1486864 | tf_op jit(solution)/shard_map/all_gather | solution.py:86
  716.0 4.3 copy.136
  720.3 85.5 %all-reduce.5.cloned.1.call-done = bf16[512,1408]{0,1:T(8,128)(2,1)} async-done(((bf16[512,1408]{0,1:T(8,128)(2,1)}), bf16[512,1408]{0,1:T(8,128)(2,1)}) %all-reduce.5.cloned.1.call-update) | async-done | bytes 1441808 | tf_op jit(solution)/shard_map/psum | solution.py:120
  809.6 29.3 %all_to_all.18 = bf16[512,3,176]{2,1,0:T(4,128)(2,1)S(1)} all-to-all(bf16[512,3,176]{2,1,0:T(4,128)(2,1)S(1)} %copy.138), channel_id=1, replica_groups=mesh['gx'=4,'gy'=8] {'gy'}, dimensions={0} | all-to-all | bytes 1081344 | tf_op jit(solution)/shard_map/all_to_all | solution.py:237
  (164 shorter events, 67.0 us)
Async XLA Ops:
  6.5 3.0 copy-start
  6.5 30.6 %all-gather.22.cloned.1.call-start = ((), (), s32[]{:S(2)}) async-start(), calls=%async_computation.3 | async-start | bytes 3604480 | tf_op jit(solution)/shard_map/all_gather | solution.py:86
  8.7 80.6 %all-gather.20.cloned.1.call-start = ((), (), s32[]{:S(2)}) async-start(), calls=%async_computation.2 | async-start | bytes 2433024 | tf_op jit(solution)/shard_map/all_gather | solution.py:155
  9.5 136.5 %all-gather.24.cloned.1.call-start = ((), (), s32[]{:S(2)}) async-start(), calls=%async_computation.4 | async-start | bytes 2433024 | tf_op jit(solution)/shard_map/all_gather | solution.py:82
  42.6 49.8 %copy-start.17 = (f32[1408]{0:T(1024)S(1)}, f32[1408]{0:T(1024)}, u32[]{:S(2)}) copy-start(f32[1408]{0:T(1024)} %param.28) | copy-start | bytes 16900
  89.3 3.0 copy-start.6
  97.3 100.2 %all-gather.26.cloned.1.call-start = ((), (), s32[]{:S(2)}) async-start(), calls=%async_computation.5 | async-start | bytes 2433024 | tf_op jit(solution)/shard_map/all_gather | solution.py:82
  148.9 71.5 %all-gather.28.cloned.1.call-start = ((), (), s32[]{:S(2)}) async-start(), calls=%async_computation.6 | async-start | bytes 2703360 | tf_op jit(solution)/shard_map/all_gather | solution.py:86
  149.5 95.3 %all-gather.30.cloned.1.call-start = ((), (), s32[]{:S(2)}) async-start(), calls=%async_computation.7 | async-start | bytes 2703360 | tf_op jit(solution)/shard_map/all_gather | solution.py:109
  150.1 94.8 %copy-start.18 = (f32[1408]{0:T(1024)S(1)}, f32[1408]{0:T(1024)}, u32[]{:S(2)}) copy-start(f32[1408]{0:T(1024)} %param.31) | copy-start | bytes 16900
  150.1 209.8 %all-reduce.3.cloned.1.call-start = ((), (), s32[]{:S(2)}) async-start(), calls=%async_computation.8 | async-start | bytes 4325376 | tf_op jit(solution)/shard_map/psum | solution.py:120
  256.7 131.5 %all-gather.32.cloned.1.call-start = ((), (), s32[]{:S(2)}) async-start(), calls=%async_computation.9 | async-start | bytes 3604480 | tf_op jit(solution)/shard_map/all_gather | solution.py:86
  259.2 197.1 %reduce-scatter.2.cloned.1.call-start = ((), (), s32[]{:S(2)}) async-start(), calls=%async_computation.10 | async-start | bytes 1622016 | tf_op jit(solution)/shard_map/reduce_scatter | solution.py:196
  272.3 2.9 copy-start.10
  275.2 208.9 %all-gather.36.cloned.1.call-start = ((), (), s32[]{:S(2)}) async-start(), calls=%async_computation.12 | async-start | bytes 3604480 | tf_op jit(solution)/shard_map/all_gather | solution.py:86
  276.6 252.6 %all-gather.34.cloned.1.call-start = ((), (), s32[]{:S(2)}) async-start(), calls=%async_computation.11 | async-start | bytes 1622016 | tf_op jit(solution)/shard_map/all_gather | solution.py:82
  370.1 4.1 copy-start.2
  374.2 14.1 %copy-start.16 = (f32[4,1408]{1,0:T(4,128)S(1)}, f32[4,1408]{1,0:T(4,128)}, u32[]{:S(2)}) copy-start(f32[4,1408]{1,0:T(4,128)} %param.34) | copy-start | bytes 67588
  392.5 66.1 %copy-start.22 = (s32[8]{0:T(128)S(1)}, s32[8]{0:T(128)}, u32[]{:S(2)}) copy-start(s32[8]{0:T(128)} %param.26) | copy-start | bytes 100
  458.4 137.9 %all-gather.38.cloned.1.call-start = ((), (), s32[]{:S(2)}) async-start(), calls=%async_computation.13 | async-start | bytes 1622016 | tf_op jit(solution)/shard_map/all_gather | solution.py:82
  460.2 70.8 %copy-start.19 = (f32[1408]{0:T(1024)S(1)}, f32[1408]{0:T(1024)}, u32[]{:S(2)}) copy-start(f32[1408]{0:T(1024)} %param.36) | copy-start | bytes 16900
  555.4 40.8 %copy-start.8 = (bf16[512,176]{0,1:T(8,128)(2,1)S(1)}, bf16[512,176]{0,1:T(8,128)(2,1)}, u32[]{:S(2)}) copy-start(bf16[512,176]{0,1:T(8,128)(2,1)} %fusion.152) | copy-start | bytes 540676
  555.4 84.9 %all-gather.40.cloned.1.call-start = ((), (), s32[]{:S(2)}) async-start(), calls=%async_computation.14 | async-start | bytes 1622016 | tf_op jit(solution)/shard_map/all_gather | solution.py:82
  563.1 36.9 %copy-start.11 = (bf16[352,3,176]{0,2,1:T(8,128)(2,1)S(1)}, bf16[352,3,176]{0,2,1:T(8,128)(2,1)}, u32[]{:S(2)}) copy-start(bf16[352,3,176]{0,2,1:T(8,128)(2,1)} %param.43) | copy-start | bytes 1115140
  598.8 88.7 %copy-start.20 = (f32[1408]{0:T(1024)S(1)}, f32[1408]{0:T(1024)}, u32[]{:S(2)}) copy-start(f32[1408]{0:T(1024)} %param.39) | copy-start | bytes 16900
  598.8 64.3 %all-gather.42.cloned.1.call-start = ((), (), s32[]{:S(2)}) async-start(), calls=%async_computation.15 | async-start | bytes 2703360 | tf_op jit(solution)/shard_map/all_gather | solution.py:86
  599.3 88.2 %all-gather.44.cloned.1.call-start = ((), (), s32[]{:S(2)}) async-start(), calls=%async_computation.16 | async-start | bytes 2703360 | tf_op jit(solution)/shard_map/all_gather | solution.py:109
  599.9 116.1 %all-gather.46.cloned.1.call-start = ((), (), s32[]{:S(2)}) async-start(), calls=%async_computation.18 | async-start | bytes 3604480 | tf_op jit(solution)/shard_map/all_gather | solution.py:86
  601.3 204.4 %all-reduce.5.cloned.1.call-start = ((), (), s32[]{:S(2)}) async-start(), calls=%async_computation.17 | async-start | bytes 2883584 | tf_op jit(solution)/shard_map/psum | solution.py:120
  696.9 108.9 %copy-start.5 = (bf16[512,1408]{0,1:T(8,128)(2,1)S(1)}, bf16[512,1408]{0,1:T(8,128)(2,1)}, u32[]{:S(2)}) copy-start(bf16[512,1408]{0,1:T(8,128)(2,1)} %all-gather.40.cloned.1.call-done) | copy-start | bytes 4325380
  720.3 87.5 %copy-start.21 = (f32[1408]{0:T(1024)S(1)}, f32[1408]{0:T(1024)}, u32[]{:S(2)}) copy-start(f32[1408]{0:T(1024)} %param.42) | copy-start | bytes 16900
  809.6 31.4 %copy-start.1 = (s32[8,2]{0,1:T(2,128)S(1)}, s32[8,2]{0,1:T(2,128)}, u32[]{:S(2)}) copy-start(s32[8,2]{0,1:T(2,128)} %param.23) | copy-start | bytes 196
  (8 other events, 17.4 us)
Sparse Core Ops, SparseCore 0:
  8.9 28.1 all-gather.21
  39.3 49.9 all-gather.19
  97.5 48.4 all-gather.23
  149.0 48.4 all-gather.25
  198.9 21.4 all-gather.27
  221.8 22.9 all-gather.29
  256.9 102.9 all-reduce.2
  361.4 26.8 all-gather.31
  391.7 64.4 reduce-scatter.1
  457.6 26.3 all-gather.35
  486.2 42.9 all-gather.33
  555.5 40.6 all-gather.37
  598.9 41.3 all-gather.39
  641.7 21.3 all-gather.41
  664.5 22.9 all-gather.43
  688.9 27.0 all-gather.45
  719.5 86.2 all-reduce.4
where the time goes:
time: 856 us; the launch traced here: 848 us
  waiting for transfers between devices  645 us (75%)
  blocking collectives  66.8 us (8%)
  local copies, waits for them, and re-layouts  51 us (6%)
  matrix products  46.8 us (5%)
  other arithmetic  22.1 us (3%)
  between operations  14.3 us (2%)
    all_gather x5, waiting for transfers between devices, spread_features(): return lax.all_gather(values, 'gy', axis=1, tiled=True)  200 us
    psum x2, waiting for transfers between devices, feed_forward(): lax.psum(partial_sum.astype(jnp.bfloat16), 'gy').astype(jnp.float32)  167 us
    all_gather x6, waiting for transfers between devices, fold_rows(): lax.all_gather(blocks, 'gx', axis=0, tiled=True)  123 us
    reduce_scatter x1, waiting for transfers between devices, per_device(): lax.psum_scatter(table_terms.astype(jnp.bfloat16), 'gy', scatter_dimensio...  56.9 us
    all_gather x2, waiting for transfers between devices, down_columns(): lax.all_gather(weight, 'gx', axis=0, tiled=True)  48.8 us
    all_gather x1, waiting for transfers between devices, per_device(): patches_full = lax.all_gather(patches, 'gy', axis=0, tiled=True)  46.8 us
    all_to_all x1, blocking collectives, per_device(): lax.all_to_all(next_local, 'gy', split_axis=0, concat_axis=2, tiled=True)  29.3 us
    dot_general x2, matrix products, down_columns(): lax.dot_general(hidden, lax.all_gather(weight, 'gx', axis=0, tiled=True),...  21.3 us
  transfers between devices with their start and end apart: 17, of which 17 were waited for; matrix products, arithmetic and copies ran while one was open for 9% of the time, Pallas kernels for 0%

commit v1 on v0

v1 whole, which is shorter than its diff:
```python
import jax
import jax.numpy as jnp
from jax import lax
from jax.experimental import pallas as pl
from jax.experimental.pallas import tpu as pltpu
from jax.sharding import PartitionSpec as P

HEAD_DIM = 88


norm_eps = 1e-06


def layer_norm(values, gain_row):
    values = values.astype(jnp.float32)
    centre = values - jnp.mean(values, axis=-1, keepdims=True)
    spread = jnp.mean(centre * centre, axis=-1, keepdims=True)
    return (centre * lax.rsqrt(spread + norm_eps) * gain_row).astype(jnp.bfloat16)


def rms_norm(values, gain_row):
    values = values.astype(jnp.float32)
    square = jnp.mean(values * values, axis=-1, keepdims=True)
    return (values * lax.rsqrt(square + norm_eps) * gain_row).astype(jnp.bfloat16)


def image_bounds(grid_rows):
    merged_count = grid_rows[:, 0] * grid_rows[:, 1]
    merged_end = jnp.cumsum(merged_count)
    return (merged_count, merged_end)


def patch_images(grid_rows, patch_slots):
    merged_count, merged_end = image_bounds(grid_rows)
    slot_index = jnp.arange(patch_slots, dtype=jnp.int32)
    return jnp.sum((slot_index[:, None] >= 4 * merged_end[None, :]).astype(jnp.int32), axis=1)


def merge_sources(grid_rows, merge_slots):
    image_count = grid_rows.shape[0]
    merged_count, merged_end = image_bounds(grid_rows)
    merged_start = merged_end - merged_count
    slot_index = jnp.arange(merge_slots, dtype=jnp.int32)
    image_of = jnp.sum((slot_index[:, None] >= merged_end[None, :]).astype(jnp.int32), axis=1)
    is_live = image_of < image_count
    picked = (
        jnp.minimum(image_of, image_count - 1)[:, None]
        == jnp.arange(image_count, dtype=jnp.int32)[None, :]
    ).astype(jnp.int32)
    col_count = jnp.sum(picked * grid_rows[None, :, 1], axis=1)
    first_slot = jnp.sum(picked * merged_start[None, :], axis=1)
    local_slot = slot_index - first_slot
    grid_row = local_slot // col_count
    grid_col = local_slot % col_count
    base_row = 4 * first_slot + 4 * grid_row * col_count + 2 * grid_col
    offsets = jnp.stack(
        [jnp.zeros_like(col_count), jnp.ones_like(col_count), 2 * col_count, 2 * col_count + 1],
        axis=1,
    )
    return jnp.where(is_live[:, None], base_row[:, None] + offsets, 0)


def request_of(index_rows, bounds):
    return jnp.sum((index_rows[:, None] >= bounds[None, :]).astype(jnp.int32), axis=1)


def local_heads(queries, key_rows, value_rows, allowed):
    scores = jnp.einsum(
        "qhe,khe->hqk", queries, key_rows, preferred_element_type=jnp.float32
    ) * HEAD_DIM ** (-0.5)
    exp_scores = jnp.where(allowed[None], jnp.exp(scores), 0.0)
    denominator = jnp.sum(exp_scores, axis=2)
    weighted = jnp.einsum(
        "hqk,khe->qhe",
        exp_scores.astype(jnp.bfloat16),
        value_rows,
        preferred_element_type=jnp.float32,
    )
    result = (weighted / denominator.T[:, :, None]).astype(jnp.bfloat16)
    return result.reshape(queries.shape[0], -1)


Z_COUNT = 4
MESH = pl.DeviceIdType.MESH


def grid_of(count):
    tall = Z_COUNT if count % Z_COUNT == 0 else 1
    return tall, count // tall


def column_parts(width):
    first = (width // 128 + 1) // 2 * 128
    return pl.ds(0, first), pl.ds(first, width - first)


def greet(places):
    barrier = pltpu.get_barrier_semaphore()
    for present, peer in places:
        @pl.when(present)
        def _():
            pl.semaphore_signal(barrier, inc=1, device_id={"gy": peer}, device_id_type=MESH)
    pl.semaphore_wait(barrier, sum(jnp.where(present, 1, 0) for present, peer in places))


def neighbours(z, x, z_count, x_count):
    return (
        (z > 0, jnp.maximum(z - 1, 0) * x_count + x),
        (z < z_count - 1, jnp.minimum(z + 1, z_count - 1) * x_count + x),
        (x > 0, z * x_count + jnp.maximum(x - 1, 0)),
        (x < x_count - 1, z * x_count + jnp.minimum(x + 1, x_count - 1)),
    )


def line_gather(count, pos, device_of, view, sends, recvs):
    last = count - 1
    for step in range(count - 1):
        moves = []
        for way in (0, 1):
            toward = 1 if way == 0 else -1
            own = pos - toward * step
            peer = pos + toward
            come = pos - toward * (step + 1)
            sending = (own >= 0) & (own <= last) & (peer >= 0) & (peer <= last)
            coming = (come >= 0) & (come <= last)
            peer = jnp.clip(peer, 0, last)

            def copy_of(index, peer=peer, way=way, step=step):
                part = view(jnp.clip(index, 0, last))
                return pltpu.make_async_remote_copy(
                    src_ref=part,
                    dst_ref=part,
                    send_sem=sends.at[way, step],
                    recv_sem=recvs.at[way, step],
                    device_id={"gy": device_of(peer)},
                    device_id_type=MESH,
                )

            @pl.when(sending)
            def _():
                copy_of(own).start()

            moves.append((sending, own, coming, come, copy_of))
        yield
        for sending, own, coming, come, copy_of in moves:
            @pl.when(coming)
            def _():
                copy_of(come).wait_recv()
        yield
        for sending, own, coming, come, copy_of in moves:
            @pl.when(sending)
            def _():
                copy_of(own).wait_send()


def chain(*lines):
    for line in lines:
        yield from line


def run_together(*lines):
    lines = list(lines)
    while lines:
        for line in list(lines):
            try:
                next(line)
            except StopIteration:
                lines.remove(line)


def gather_kernel(z_count, x_count, block, out, *sems):
    me = lax.axis_index("gy")
    z, x = me // x_count, me % x_count
    greet(neighbours(z, x, z_count, x_count))
    out[z, x] = block[...]
    left, right = column_parts(block.shape[1])

    def along_z(k):
        return k * x_count + x

    def along_x(k):
        return z * x_count + k

    run_together(
        chain(
            line_gather(z_count, z, along_z, lambda k: out.at[k, x, :, left], sems[0], sems[1]),
            line_gather(
                x_count, x, along_x, lambda k: out.at[:, k, :, left], sems[2], sems[3]
            ),
        ),
        chain(
            line_gather(x_count, x, along_x, lambda k: out.at[z, k, :, right], sems[4], sems[5]),
            line_gather(
                z_count, z, along_z, lambda k: out.at[k, :, :, right], sems[6], sems[7]
            ),
        ),
    )


def line_reduce(count, pos, device_of, own, store, outgoing, incoming, sends, recvs):
    last = count - 1
    for step in range(count - 1):
        moves = []
        for way in (0, 1):
            toward = 1 if way == 0 else -1
            dest = last - step if way == 0 else step
            peer = jnp.clip(pos + toward, 0, last)
            sending = pos < dest if way == 0 else pos > dest
            fed = (pos > 0) if way == 0 else (pos < last)
            coming = fed & ((pos <= dest) if way == 0 else (pos >= dest))
            copy = pltpu.make_async_remote_copy(
                src_ref=outgoing.at[way, step],
                dst_ref=incoming.at[way, step],
                send_sem=sends.at[way, step],
                recv_sem=recvs.at[way, step],
                device_id={"gy": device_of(peer)},
                device_id_type=MESH,
            )
            moves.append((sending, fed, coming, copy, dest, way))
        for sending, fed, coming, copy, dest, way in moves:
            @pl.when(coming)
            def _():
                copy.wait_recv()

            @pl.when(sending & fed)
            def _():
                outgoing[way, step] = (own(dest) + incoming[way, step].astype(jnp.float32)).astype(
                    jnp.bfloat16
                )

            @pl.when(sending & jnp.logical_not(fed))
            def _():
                outgoing[way, step] = own(dest).astype(jnp.bfloat16)

            @pl.when(sending)
            def _():
                copy.start()
        yield
        for sending, fed, coming, copy, dest, way in moves:
            @pl.when(sending)
            def _():
                copy.wait_send()
    store(own(pos))
    for way in (0, 1):
        step_of = last - pos if way == 0 else pos

        @pl.when(pos > 0 if way == 0 else pos < last)
        def _():
            kept = jnp.clip(step_of, 0, max(last - 1, 0))
            store(None, incoming[way, kept].astype(jnp.float32))
    yield


def reduce_kernel(z_count, x_count, terms, out, sum_l, sum_r, total_l, total_r, *rest):
    bufs, sems = rest[:8], rest[8:]
    me = lax.axis_index("gy")
    z, x = me // x_count, me % x_count
    greet(neighbours(z, x, z_count, x_count))
    left, right = column_parts(terms.shape[3])

    def along_z(k):
        return k * x_count + x

    def along_x(k):
        return z * x_count + k

    def keep(ref):
        def store(first, more=None):
            if more is None:
                ref[...] = first
            else:
                ref[...] += more

        return store

    run_together(
        chain(
            line_reduce(
                x_count, x, along_x, lambda k: terms[:, k, :, left].astype(jnp.float32),
                keep(sum_l), bufs[0], bufs[1], sems[0], sems[1],
            ),
            line_reduce(
                z_count, z, along_z, lambda k: sum_l[k], keep(total_l),
                bufs[2], bufs[3], sems[2], sems[3],
            ),
        ),
        chain(
            line_reduce(
                z_count, z, along_z, lambda k: terms[k, :, :, right].astype(jnp.float32),
                keep(sum_r), bufs[4], bufs[5], sems[4], sems[5],
            ),
            line_reduce(
                x_count, x, along_x, lambda k: sum_r[k], keep(total_r),
                bufs[6], bufs[7], sems[6], sems[7],
            ),
        ),
    )
    out[:, left] = total_l[...]
    out[:, right] = total_r[...]


def swap_kernel(count, blocks, out, sends, recvs):
    me = lax.axis_index("gy")
    barrier = pltpu.get_barrier_semaphore()
    for shift in range(1, count):
        peer = lax.rem(me + shift, count)
        pl.semaphore_signal(barrier, inc=1, device_id={"gy": peer}, device_id_type=MESH)
    pl.semaphore_wait(barrier, count - 1)
    copies = []
    for shift in range(1, count):
        peer = lax.rem(me + shift, count)
        copy = pltpu.make_async_remote_copy(
            src_ref=blocks.at[peer],
            dst_ref=out.at[me],
            send_sem=sends.at[shift - 1],
            recv_sem=recvs.at[shift - 1],
            device_id={"gy": peer},
            device_id_type=MESH,
        )
        copy.start()
        copies.append(copy)
    out[me] = blocks[me]
    for copy in copies:
        copy.wait_recv()
    for copy in copies:
        copy.wait_send()


def call(body, out_shape, scratch, identity, name, size):
    whole = pl.BlockSpec(memory_space=pltpu.VMEM)
    return pl.pallas_call(
        body,
        out_shape=out_shape,
        in_specs=[whole],
        out_specs=whole,
        scratch_shapes=scratch,
        name=name,
        cost_estimate=pl.CostEstimate(flops=0, bytes_accessed=size, transcendentals=0),
        compiler_params=pltpu.CompilerParams(
            collective_id=identity, has_side_effects=True, vmem_limit_bytes=48 * 1024 * 1024
        ),
    )


def pair(count):
    sems = pltpu.SemaphoreType.DMA((2, max(count - 1, 1)))
    return [sems, sems]


def gather_rows(block, identity):
    z_count, x_count = grid_of(lax.axis_size("gy"))
    rows, width = block.shape
    scratch = pair(z_count) + pair(x_count) + pair(x_count) + pair(z_count)
    out = call(
        lambda *refs: gather_kernel(z_count, x_count, *refs),
        jax.ShapeDtypeStruct((z_count, x_count, rows, width), jnp.bfloat16),
        scratch, identity, "gather_rows", 60000000,
    )(block)
    return out.reshape(z_count * x_count * rows, width)


def sum_rows(terms, identity):
    z_count, x_count = grid_of(lax.axis_size("gy"))
    width = terms.shape[1]
    rows = terms.shape[0] // (z_count * x_count)
    left, right = column_parts(width)
    l_size, r_size = left.size, right.size

    def slots(count, *shape):
        slot = pltpu.VMEM((2, max(count - 1, 1)) + shape, jnp.bfloat16)
        return [slot, slot]

    scratch = (
        [
            pltpu.VMEM((z_count, rows, l_size), jnp.float32),
            pltpu.VMEM((x_count, rows, r_size), jnp.float32),
            pltpu.VMEM((rows, l_size), jnp.float32),
            pltpu.VMEM((rows, r_size), jnp.float32),
        ]
        + slots(x_count, z_count, rows, l_size)
        + slots(z_count, rows, l_size)
        + slots(z_count, x_count, rows, r_size)
        + slots(x_count, rows, r_size)
        + pair(x_count) + pair(z_count) + pair(z_count) + pair(x_count)
    )
    return call(
        lambda *refs: reduce_kernel(z_count, x_count, *refs),
        jax.ShapeDtypeStruct((rows, width), jnp.float32),
        scratch, identity, "sum_rows", 60000000,
    )(terms.reshape(z_count, x_count, rows, width))


def swap_to_rows(values, identity):
    count = lax.axis_size("gy")
    rows, width = values.shape[0] // count, values.shape[1]
    sems = pltpu.SemaphoreType.DMA((count - 1,))
    out = call(
        lambda *refs: swap_kernel(count, *refs),
        jax.ShapeDtypeStruct((count, rows, width), jnp.bfloat16),
        [sems, sems], identity, "swap_to_rows", 20000000,
    )(values.reshape(count, rows, width))
    return out.transpose(1, 0, 2)


def full_weight(weight):
    rows, width = weight.shape
    everywhere = lax.all_gather(weight, ("gx", "gy"), axis=0, tiled=False)
    gx_count, gy_count = lax.axis_size("gx"), lax.axis_size("gy")
    return (
        everywhere.reshape(gx_count, gy_count, rows, width)
        .transpose(0, 2, 1, 3)
        .reshape(gx_count * rows, gy_count * width)
    )


def weight_columns(weight):
    return lax.all_gather(weight.reshape(weight.shape[0], -1), "gx", axis=0, tiled=True)


def dense(rows, weight):
    return jnp.dot(rows, weight, preferred_element_type=jnp.float32)


def feed_forward(normed_full, fc_in, fc_back, identity):
    hidden = jax.nn.gelu(dense(normed_full, fc_in), approximate=False).astype(jnp.bfloat16)
    partial_sum = lax.dot_general(
        hidden, fc_back, (((1,), (1,)), ((), ())), preferred_element_type=jnp.float32
    )
    return sum_rows(partial_sum.astype(jnp.bfloat16), identity)


def per_device(
    patches,
    grids,
    text_ids,
    positions,
    lengths,
    text_table,
    vit_norm1,
    vit_qkv,
    vit_out,
    vit_norm2,
    vit_fc1,
    vit_fc2,
    merge_norm,
    merge_proj,
    dec_norm1,
    dec_qkv,
    dec_out,
    dec_norm2,
    dec_fc1,
    dec_fc2,
    next_norm,
    next_qkv,
):
    gx_count = lax.axis_size("gx")
    gx_index = lax.axis_index("gx")
    gy_count = lax.axis_size("gy")
    gy_index = lax.axis_index("gy")
    per_group = grids.shape[0] // gx_count
    own_grids = lax.dynamic_slice_in_dim(grids, gx_index * per_group, per_group, 0)
    local_width = vit_qkv.shape[2]
    head_count = local_width // HEAD_DIM
    vit_qkv, vit_fc1, vit_fc2, merge_proj, dec_qkv, dec_fc1, dec_fc2, next_qkv = [
        weight_columns(weight)
        for weight in (vit_qkv, vit_fc1, vit_fc2, merge_proj, dec_qkv, dec_fc1, dec_fc2, next_qkv)
    ]
    vit_out, dec_out = full_weight(vit_out), full_weight(dec_out)

    patches_full = gather_rows(patches, 0)
    patch_slots, full_width = patches_full.shape
    merge_slots = positions.shape[0] // gx_count
    sources = merge_sources(own_grids, merge_slots).reshape(merge_slots * 4)
    slot_index = jnp.arange(patch_slots, dtype=jnp.int32)
    chosen = (sources[:, None] == slot_index[None, :]).astype(jnp.bfloat16)
    ordered = dense(chosen, patches_full).astype(jnp.bfloat16)
    triple = dense(layer_norm(ordered, vit_norm1), vit_qkv).astype(jnp.bfloat16)
    triple = triple.reshape(patch_slots, 3, head_count, HEAD_DIM)
    image_ids = jnp.sum(
        (sources[:, None] >= 4 * image_bounds(own_grids)[1][None, :]).astype(jnp.int32), axis=1
    )
    is_key = slot_index < 4 * jnp.sum(own_grids[:, 0] * own_grids[:, 1])
    attended = local_heads(
        triple[:, 0],
        triple[:, 1],
        triple[:, 2],
        (image_ids[:, None] == image_ids[None, :]) & is_key[None, :],
    )
    own_rows = patch_slots // gy_count
    patches_own = lax.dynamic_slice_in_dim(ordered, gy_index * own_rows, own_rows, 0)
    attended_own = swap_to_rows(attended, 1).reshape(own_rows, full_width)
    vit_mid = (patches_own.astype(jnp.float32) + dense(attended_own, vit_out)).astype(jnp.bfloat16)
    vit_normed = gather_rows(layer_norm(vit_mid, vit_norm2), 2)
    summed = feed_forward(vit_normed, vit_fc1, vit_fc2, 3)
    vit_final = (vit_mid.astype(jnp.float32) + summed).astype(jnp.bfloat16)
    merged = vit_final.astype(jnp.float32).reshape(own_rows // 4, 4, full_width)
    centre = merged - jnp.mean(merged, axis=(1, 2), keepdims=True)
    spread = jnp.mean(centre * centre, axis=(1, 2), keepdims=True)
    merged_normed = (centre * lax.rsqrt(spread + norm_eps) * merge_norm).astype(jnp.bfloat16)
    merged_full = gather_rows(merged_normed.reshape(own_rows, full_width), 4)
    products = dense(merged_full, merge_proj).reshape(merge_slots, 4, 4 * local_width)
    projected = products[:, 0, :local_width]
    for k in range(1, 4):
        projected = projected + products[:, k, k * local_width : (k + 1) * local_width]
    projected = projected.astype(jnp.bfloat16)

    seq_slots = text_ids.shape[0]
    seq_rows = seq_slots // gy_count
    seq_index = gx_index * seq_slots + jnp.arange(seq_slots, dtype=jnp.int32)
    matches = positions[None, :] == seq_index[:, None]
    all_projected = lax.all_gather(projected, "gx", axis=0, tiled=True)
    placed = dense(matches.astype(jnp.bfloat16), all_projected).astype(jnp.bfloat16)
    placed_own = swap_to_rows(placed, 5).reshape(seq_rows, full_width)
    vocab_rows = text_table.shape[0]
    shifted_ids = text_ids - gy_index * vocab_rows
    inside = (shifted_ids >= 0) & (shifted_ids < vocab_rows)
    looked_up = jnp.take(text_table, jnp.clip(shifted_ids, 0, vocab_rows - 1), axis=0)
    table_terms = jnp.where(inside[:, None], looked_up, jnp.bfloat16(0))
    text_own = sum_rows(table_terms, 6).astype(jnp.bfloat16)
    is_image = lax.dynamic_slice_in_dim(
        jnp.any(matches, axis=1), gy_index * seq_rows, seq_rows, 0
    )
    embedded = jnp.where(is_image[:, None], placed_own, text_own)

    dec_normed = gather_rows(rms_norm(embedded, dec_norm1), 7)
    dec_triple = dense(dec_normed, dec_qkv).astype(jnp.bfloat16)
    queries = dec_triple[:, :local_width].reshape(seq_slots, head_count, HEAD_DIM)
    bounds = jnp.cumsum(lengths)
    own_request = request_of(seq_index, bounds)
    pairs = lax.all_gather(dec_triple[:, local_width:], "gx", axis=0, tiled=True)
    key_count = pairs.shape[0]
    pairs = pairs.reshape(key_count, 2, head_count, HEAD_DIM)
    key_index = jnp.arange(key_count, dtype=jnp.int32)
    allowed = (request_of(key_index, bounds)[None, :] == own_request[:, None]) & (
        key_index[None, :] <= seq_index[:, None]
    )
    dec_attended = local_heads(queries, pairs[:, 0], pairs[:, 1], allowed)
    dec_own = swap_to_rows(dec_attended, 8).reshape(seq_rows, full_width)
    dec_mid = (embedded.astype(jnp.float32) + dense(dec_own, dec_out)).astype(jnp.bfloat16)
    mid_normed = gather_rows(rms_norm(dec_mid, dec_norm2), 9)
    summed = feed_forward(mid_normed, dec_fc1, dec_fc2, 10)
    dec_final = (dec_mid.astype(jnp.float32) + summed).astype(jnp.bfloat16)
    next_normed = gather_rows(rms_norm(dec_final, next_norm), 11)
    next_local = dense(next_normed, next_qkv).astype(jnp.bfloat16)
    next_own = swap_to_rows(next_local, 12).reshape(seq_rows, gy_count, 3, local_width)
    return next_own.transpose(0, 2, 1, 3).reshape(seq_rows, 3, full_width)


def solution(mesh):
    placed = (
        P(("gx", "gy"), None),
        P(),
        P("gx"),
        P(),
        P(),
        P("gy", None),
        P(),
        P("gx", None, "gy"),
        P("gx", "gy"),
        P(),
        P("gx", "gy"),
        P("gx", "gy"),
        P(),
        P("gx", None, "gy"),
        P(),
        P("gx", None, "gy"),
        P("gx", "gy"),
        P(),
        P("gx", "gy"),
        P("gx", "gy"),
        P(),
        P("gx", None, "gy"),
    )
    return jax.shard_map(
        per_device,
        mesh=mesh,
        in_specs=placed,
        out_specs=P(("gx", "gy"), None, None),
        check_vma=False,
    )
```

time: 856 us -> 704 us (0.82)
  waiting for transfers between devices: 645 us -> 8.29 us
  Pallas kernels: 0 us -> 535 us
  blocking collectives: 66.8 us -> 11.5 us
  local copies, waits for them, and re-layouts: 51 us -> 68.2 us
  other arithmetic: 22.1 us -> 7.62 us
    pallas_call x0 -> x13, Pallas kernels: none -> 535 us  [the longest x3 322 us: sum_rows(): call(lambda *refs: reduce_kernel(z_count, x_count, *refs), jax.ShapeDtype...]
    all_gather x14 -> x11, waiting for transfers between devices: 418 us -> 2.51 us  [the longest x8 2.51 us: weight_columns(): lax.all_gather(weight.reshape(weight.shape[0], -1), 'gx', axis=0, tiled=T...]
    psum x2 -> x0, waiting for transfers between devices: 167 us -> none  [feed_forward(): lax.psum(partial_sum.astype(jnp.bfloat16), 'gy').astype(jnp.float32)]
    reduce_scatter x1 -> x0, waiting for transfers between devices: 56.9 us -> none  [per_device(): lax.psum_scatter(table_terms.astype(jnp.bfloat16), 'gy', scatter_dimensio...]
    reshape x0 -> x10, local copies, waits for them, and re-layouts: none -> 36.3 us  [the longest x2 16.7 us: full_weight(): return everywhere.reshape(gx_count, gy_count, rows, width).transpose(0, 2...]
    all_to_all x1 -> x0, blocking collectives: 29.3 us -> none  [per_device(): lax.all_to_all(next_local, 'gy', split_axis=0, concat_axis=2, tiled=True)]
    all_gather x5 -> x1, blocking collectives: 37.5 us -> 11.5 us  [per_device(): all_projected = lax.all_gather(projected, 'gx', axis=0, tiled=True)]
    dot_general x11 -> x10, matrix products: 43.5 us -> 40.8 us  [the longest x2 21.5 us: feed_forward(): lax.dot_general(hidden, fc_back, (((1,), (1,)), ((), ())), preferred_elem...]
  transfers between devices with their start and end apart: 17 -> 11, of which waited for: 17 -> 1; matrix products, arithmetic and copies ran while one was open for 9% -> 16% of each run, Pallas kernels for 0% -> 57%
where the time goes in v1:
time: 704 us; the launch traced here: 695 us
  Pallas kernels  535 us (76%)
  local copies, waits for them, and re-layouts  68.2 us (10%)
  matrix products  49.6 us (7%)
  between operations  15 us (2%)
  blocking collectives  11.5 us (2%)
  waiting for transfers between devices  8.29 us (1%)
  other arithmetic  7.62 us (1%)
    pallas_call x3, Pallas kernels, sum_rows(): call(lambda *refs: reduce_kernel(z_count, x_count, *refs), jax.ShapeDtype...  322 us
    pallas_call x6, Pallas kernels, gather_rows(): call(lambda *refs: gather_kernel(z_count, x_count, *refs), jax.ShapeDtype...  169 us
    pallas_call x4, Pallas kernels, swap_to_rows(): call(lambda *refs: swap_kernel(count, *refs), jax.ShapeDtypeStruct((count...  43.8 us
    dot_general x2, matrix products, feed_forward(): lax.dot_general(hidden, fc_back, (((1,), (1,)), ((), ())), preferred_elem...  21.5 us
    dot_general x8, matrix products, dense(): return jnp.dot(rows, weight, preferred_element_type=jnp.float32)  19.3 us
    reshape x2, local copies, waits for them, and re-layouts, full_weight(): return everywhere.reshape(gx_count, gy_count, rows, width).transpose(0, 2...  16.7 us
    reshape x2, local copies, waits for them, and re-layouts, full_weight(): everywhere.reshape(gx_count, gy_count, rows, width).transpose(0, 2, 1, 3)  15.4 us
  transfers between devices with their start and end apart: 11, of which 1 were waited for; matrix products, arithmetic and copies ran while one was open for 16% of the time, Pallas kernels for 57%

profile of v1, /device:TPU:8, one launch (start us, length us, event | category | flops | bytes accessed | tf_op | source)
XLA Modules:
  0.0 695.4 jit_solution(17473670868929199435)
XLA Ops:
  14.2 34.6 %gather_rows.6 = bf16[4,2,96,1408]{3,2,1,0:T(8,128)(2,1)S(1)} custom-call(bf16[96,1408]{1,0:T(8,128)(2,1)S(1)} %copy-done.3), custom_call_target="tpu_custom_call" | custom-call | bytes 60000000 | tf_op jit(solution)/shard_map/gather_rows/pallas_call | solution.py:354
  48.8 2.1 convert_reduce_fusion
  55.0 9.0 %gather_fusion = bf16[512,1408]{1,0:T(8,128)(2,1)S(1)} fusion(bf16[4000,1408]{1,0:T(8,128)(2,1)} %param.27, s32[1024]{0:T(1024)S(1)} %pad_clamp_fusion), kind=kCustom, calls=%fused_computation | custom fusion | bytes 2885632 | tf_op jit(solution)/shard_map/jit(_take)/gather | solution.py:517
  64.3 105.5 %sum_rows.4 = f32[64,1408]{1,0:T(8,128)S(1)} custom-call(bf16[4,2,64,1408]{3,2,1,0:T(8,128)(2,1)S(1)} %select_select_fusion.refs_0_), custom_call_target="tpu_custom_call" | custom-call | bytes 60000000 | tf_op jit(solution)/shard_map/sum_rows/pallas_call | solution.py:386
  171.5 2.1 copy.86
  175.0 3.3 fusion.52
  181.6 8.4 %swap_to_rows.4 = bf16[8,96,176]{2,1,0:T(8,128)(2,1)S(1)} custom-call(bf16[8,96,176]{2,1,0:T(8,128)(2,1)S(1)} %copy.88.refs_0_), custom_call_target="tpu_custom_call" | custom-call | bytes 20000000 | tf_op jit(solution)/shard_map/swap_to_rows/pallas_call | solution.py:397
  190.7 2.1 copy.95
  194.7 7.6 %copy.109 = bf16[4,8,352,176]{2,0,3,1:T(4,128)(2,1)} copy(bf16[4,8,352,176]{2,3,1,0:T(8,128)(2,1)} %bitcast.144) | data formatting | bytes 7929856 | tf_op jit(solution)/shard_map/reshape | solution.py:410
  202.3 8.6 %reshape.418 = bf16[1408,1408]{0,1:T(8,128)(2,1)} reshape(bf16[4,352,8,176]{1,0,3,2:T(4,128)(2,1)} %bitcast.140) | data formatting | bytes 7929856 | tf_op jit(solution)/shard_map/reshape | solution.py:412
  210.9 3.5 fusion.224
  214.8 35.3 %gather_rows.7 = bf16[4,2,96,1408]{3,2,1,0:T(8,128)(2,1)S(1)} custom-call(bf16[96,1408]{1,0:T(8,128)(2,1)S(1)} %multiply_convert_fusion.refs_0_), custom_call_target="tpu_custom_call" | custom-call | bytes 60000000 | tf_op jit(solution)/shard_map/gather_rows/pallas_call | solution.py:354
  250.2 12.9 %convolution_convert_fusion = bf16[768,1408]{1,0:T(8,128)(2,1)} fusion(bf16[1408,768]{1,0:T(8,128)(2,1)} %all-gather.22.cloned.1.call-done, bf16[768,1408]{1,0:T(8,128)(2,1)S(1)} %bitcast.129, bf16[1408,768]{1,0:T(8,128)(2,1)} %all-gather.20.cloned.1.call-done), kind=kOutput, calls=%fused_computation.21 | convolution fusion | flops 3361308672 | bytes 8650752 | tf_op jit(solution)/shard_map/dot_general | solution.py:426
  264.7 116.3 %sum_rows.3 = f32[96,1408]{1,0:T(8,128)S(1)} custom-call(bf16[4,2,96,1408]{3,2,1,0:T(8,128)(2,1)S(1)} %bitcast.131), custom_call_target="tpu_custom_call" | custom-call | bytes 60000000 | tf_op jit(solution)/shard_map/sum_rows/pallas_call | solution.py:386
  382.4 25.3 %gather_rows.8 = bf16[4,2,96,1408]{3,2,1,0:T(8,128)(2,1)S(1)} custom-call(bf16[96,1408]{1,0:T(8,128)(2,1)S(1)} %fusion.146.refs_0_), custom_call_target="tpu_custom_call" | custom-call | bytes 60000000 | tf_op jit(solution)/shard_map/gather_rows/pallas_call | solution.py:354
  407.8 2.1 dot_general.57
  409.8 4.2 fusion.34
  414.3 11.5 %all-gather.1 = bf16[768,1,176]{2,0,1:T(8,128)(2,1)S(1)} all-gather(bf16[192,1,176]{2,0,1:T(8,128)(2,1)S(1)} %fusion.155), channel_id=3, replica_groups=mesh['gx'=4,'gy'=8] {'gx'}, dimensions={0}, use_global_device_ids=true | all-gather | bytes 337920 | tf_op jit(solution)/shard_map/all_gather | solution.py:511
  426.6 11.8 %swap_to_rows.5 = bf16[8,64,176]{2,1,0:T(8,128)(2,1)S(1)} custom-call(bf16[8,64,176]{2,1,0:T(8,128)(2,1)S(1)} %bitcast.137), custom_call_target="tpu_custom_call" | custom-call | bytes 20000000 | tf_op jit(solution)/shard_map/swap_to_rows/pallas_call | solution.py:397
  439.2 24.4 %gather_rows.9 = bf16[4,2,64,1408]{3,2,1,0:T(8,128)(2,1)S(1)} custom-call(bf16[64,1408]{1,0:T(8,128)(2,1)S(1)} %fusion.153.refs_0_), custom_call_target="tpu_custom_call" | custom-call | bytes 60000000 | tf_op jit(solution)/shard_map/gather_rows/pallas_call | solution.py:354
  473.2 7.8 %copy.108 = bf16[4,8,352,176]{2,0,3,1:T(4,128)(2,1)} copy(bf16[4,8,352,176]{2,3,1,0:T(8,128)(2,1)} %bitcast.143) | data formatting | bytes 7929856 | tf_op jit(solution)/shard_map/reshape | solution.py:410
  481.0 8.2 %reshape.432 = bf16[1408,1408]{0,1:T(8,128)(2,1)} reshape(bf16[4,352,8,176]{1,0,3,2:T(4,128)(2,1)} %bitcast.141) | data formatting | bytes 7929856 | tf_op jit(solution)/shard_map/reshape | solution.py:412
  489.2 4.1 fusion
  493.3 2.1 fusion.99
  495.8 9.8 %swap_to_rows.6 = bf16[8,64,176]{2,1,0:T(8,128)(2,1)S(1)} custom-call(bf16[8,64,176]{2,1,0:T(8,128)(2,1)S(1)} %reshape_reshape.7.refs_0_), custom_call_target="tpu_custom_call" | custom-call | bytes 20000000 | tf_op jit(solution)/shard_map/swap_to_rows/pallas_call | solution.py:397
  506.0 3.5 multiply_reduce_fusion.1
  509.7 23.5 %gather_rows.10 = bf16[4,2,64,1408]{3,2,1,0:T(8,128)(2,1)S(1)} custom-call(bf16[64,1408]{1,0:T(8,128)(2,1)S(1)} %multiply_convert_fusion.1.refs_0_), custom_call_target="tpu_custom_call" | custom-call | bytes 60000000 | tf_op jit(solution)/shard_map/gather_rows/pallas_call | solution.py:354
  533.2 2.4 all-gather.30.cloned.1.call-done
  535.6 8.5 %convolution_convert_fusion.2 = bf16[512,1408]{1,0:T(8,128)(2,1)S(1)} fusion(bf16[1408,768]{1,0:T(8,128)(2,1)} %all-gather.30.cloned.1.call-done, bf16[512,1408]{1,0:T(8,128)(2,1)S(1)} %bitcast.133, bf16[1408,768]{1,0:T(8,128)(2,1)} %all-gather.28.cloned.1.call-done), kind=kOutput, calls=%fused_computation.23 | convolution fusion | flops 2240872448 | bytes 7208960 | tf_op jit(solution)/shard_map/dot_general | solution.py:426
  544.2 99.8 %sum_rows.5 = f32[64,1408]{1,0:T(8,128)S(1)} custom-call(bf16[4,2,64,1408]{3,2,1,0:T(8,128)(2,1)S(1)} %bitcast.134), custom_call_target="tpu_custom_call" | custom-call | bytes 60000000 | tf_op jit(solution)/shard_map/sum_rows/pallas_call | solution.py:386
  644.3 26.3 %gather_rows.11 = bf16[4,2,64,1408]{3,2,1,0:T(8,128)(2,1)S(1)} custom-call(bf16[64,1408]{1,0:T(8,128)(2,1)S(1)} %fusion.150.refs_0_), custom_call_target="tpu_custom_call" | custom-call | bytes 60000000 | tf_op jit(solution)/shard_map/gather_rows/pallas_call | solution.py:354
  671.9 13.8 %swap_to_rows.7 = bf16[8,64,528]{2,1,0:T(8,128)(2,1)S(1)} custom-call(bf16[8,64,528]{2,1,0:T(8,128)(2,1)S(1)} %bitcast.127), custom_call_target="tpu_custom_call" | custom-call | bytes 20000000 | tf_op jit(solution)/shard_map/swap_to_rows/pallas_call | solution.py:397
  (164 shorter events, 40.0 us)
Async XLA Ops:
  6.5 6.1 copy-start
  6.5 3.4 copy-start.10
  6.5 164.9 %all-gather.32.cloned.1.call-start = ((), (), s32[]{:S(2)}) async-start(), calls=%async_computation.6 | async-start | bytes 2027520 | tf_op jit(solution)/shard_map/all_gather | solution.py:417
  6.5 7.6 %copy-start.3 = (bf16[96,1408]{1,0:T(8,128)(2,1)S(1)}, bf16[96,1408]{1,0:T(8,128)(2,1)}, u32[]{:S(2)}) copy-start(bf16[96,1408]{1,0:T(8,128)(2,1)} %refs_0_.1) | copy-start | bytes 811012
  7.3 183.4 %all-gather.36.cloned.1.call-start = ((), (), s32[]{:S(2)}) async-start(), calls=%async_computation.8 | async-start | bytes 2027520 | tf_op jit(solution)/shard_map/all_gather | solution.py:417
  8.0 186.7 %all-gather.34.cloned.1.call-start = ((), (), s32[]{:S(2)}) async-start(), calls=%async_computation.7 | async-start | bytes 4460544 | tf_op jit(solution)/shard_map/all_gather | solution.py:407
  8.7 241.4 %all-gather.20.cloned.1.call-start = ((), (), s32[]{:S(2)}) async-start(), calls=%async_computation | async-start | bytes 2703360 | tf_op jit(solution)/shard_map/all_gather | solution.py:417
  9.3 240.9 %all-gather.22.cloned.1.call-start = ((), (), s32[]{:S(2)}) async-start(), calls=%async_computation.1 | async-start | bytes 2703360 | tf_op jit(solution)/shard_map/all_gather | solution.py:417
  9.9 399.9 %all-gather.24.cloned.1.call-start = ((), (), s32[]{:S(2)}) async-start(), calls=%async_computation.2 | async-start | bytes 2703360 | tf_op jit(solution)/shard_map/all_gather | solution.py:417
  11.0 458.1 %all-gather.40.cloned.1.call-start = ((), (), s32[]{:S(2)}) async-start(), calls=%async_computation.10 | async-start | bytes 2027520 | tf_op jit(solution)/shard_map/all_gather | solution.py:417
  11.8 461.5 %all-gather.38.cloned.1.call-start = ((), (), s32[]{:S(2)}) async-start(), calls=%async_computation.9 | async-start | bytes 4460544 | tf_op jit(solution)/shard_map/all_gather | solution.py:407
  12.5 476.7 %all-gather.26.cloned.1.call-start = ((), (), s32[]{:S(2)}) async-start(), calls=%async_computation.3 | async-start | bytes 1802240 | tf_op jit(solution)/shard_map/all_gather | solution.py:530
  50.9 1.4 copy-start.4
  50.9 2.7 copy-start.11
  50.9 3.9 copy-start.17
  64.0 107.1 %copy-start.16 = (s32[768]{0:T(1024)S(1)}, s32[768]{0:T(1024)}, u32[]{:S(2)}) copy-start(s32[768]{0:T(1024)} %param.25) | copy-start | bytes 9220
  173.6 1.4 copy-start.19
  175.0 3.3 copy-start.8
  210.9 3.8 copy-start.12
  263.1 1.6 copy-start.2
  264.7 117.5 %copy-start.5 = (f32[96,1408]{1,0:T(8,128)S(1)}, f32[96,1408]{1,0:T(8,128)}, u32[]{:S(2)}) copy-start(f32[96,1408]{1,0:T(8,128)} %mul.306) | copy-start | bytes 1622020
  414.3 24.8 %copy-start.14 = (f32[1408]{0:T(1024)S(1)}, f32[1408]{0:T(1024)}, u32[]{:S(2)}) copy-start(f32[1408]{0:T(1024)} %param.36) | copy-start | bytes 16900
  426.6 37.0 %copy-start.6 = (bf16[1408,528]{0,1:T(8,128)(2,1)S(1)}, bf16[1408,528]{0,1:T(8,128)(2,1)}, u32[]{:S(2)}) copy-start(bf16[1408,528]{0,1:T(8,128)(2,1)} %reshape.459) | copy-start | bytes 4460548
  465.4 2.1 copy-start.20
  466.2 67.0 %all-gather.28.cloned.1.call-start = ((), (), s32[]{:S(2)}) async-start(), calls=%async_computation.4 | async-start | bytes 2703360 | tf_op jit(solution)/shard_map/all_gather | solution.py:417
  466.8 68.8 %all-gather.30.cloned.1.call-start = ((), (), s32[]{:S(2)}) async-start(), calls=%async_computation.5 | async-start | bytes 2703360 | tf_op jit(solution)/shard_map/all_gather | solution.py:417
  481.0 8.2 %slice-start = ((bf16[512,528]{0,1:T(8,128)(2,1)}), bf16[512,176]{0,1:T(8,128)(2,1)S(1)}, s32[]{:S(2)}) async-start(bf16[512,528]{0,1:T(8,128)(2,1)} %copy-done.9), calls=%async_computation.11 | async-start | bytes 360448 | tf_op jit(solution)/shard_map/slice | solution.py:527
  489.2 4.1 copy-start.18
  506.0 3.6 copy-start.13
  544.1 100.0 %copy-start.15 = (f32[1408]{0:T(1024)S(1)}, f32[1408]{0:T(1024)}, u32[]{:S(2)}) copy-start(f32[1408]{0:T(1024)} %param.42) | copy-start | bytes 16900
  544.1 126.4 %copy-start.7 = (bf16[1408,528]{0,1:T(8,128)(2,1)S(1)}, bf16[1408,528]{0,1:T(8,128)(2,1)}, u32[]{:S(2)}) copy-start(bf16[1408,528]{0,1:T(8,128)(2,1)} %reshape.463) | copy-start | bytes 4460548
  685.8 2.8 copy-start.1
  (1 other events, 0.8 us)
Sparse Core Ops, SparseCore 0:
  8.9 21.0 all-gather.31
  31.6 19.9 all-gather.35
  54.6 63.2 all-gather.33
  119.2 21.5 all-gather.19
  142.3 22.9 all-gather.21
  166.7 22.9 all-gather.23
  191.2 19.9 all-gather.39
  214.2 65.7 all-gather.37
  466.4 20.2 all-gather.25
  488.0 22.9 all-gather.27
  512.6 22.9 all-gather.29

commit v2 on v1

--- a/solution.py
+++ b/solution.py
@@ -89,8 +89,9 @@
     return tall, count // tall
 
 
-def column_parts(width):
-    first = (width // 128 + 1) // 2 * 128
+def column_parts(width, z_count, x_count):
+    tiles = width // 128
+    first = (tiles * 5 // 6 if 2 * x_count <= z_count else (tiles + 1) // 2) * 128
     return pl.ds(0, first), pl.ds(first, width - first)
 
 
@@ -112,8 +113,9 @@
     )
 
 
-def line_gather(count, pos, device_of, view, sends, recvs):
+def line_gather(count, pos, device_of, view, sends, recvs, enabled=None, arrived=None):
     last = count - 1
+    sent = []
     for step in range(count - 1):
         moves = []
         for way in (0, 1):
@@ -123,6 +125,8 @@
             come = pos - toward * (step + 1)
             sending = (own >= 0) & (own <= last) & (peer >= 0) & (peer <= last)
             coming = (come >= 0) & (come <= last)
+            if enabled is not None:
+                sending, coming = sending & enabled, coming & enabled
             peer = jnp.clip(peer, 0, last)
 
             def copy_of(index, peer=peer, way=way, step=step):
@@ -130,8 +134,8 @@
                 return pltpu.make_async_remote_copy(
                     src_ref=part,
                     dst_ref=part,
-                    send_sem=sends.at[way, step],
-                    recv_sem=recvs.at[way, step],
+                    send_sem=sends(way, step),
+                    recv_sem=recvs(way, step),
                     device_id={"gy": device_of(peer)},
                     device_id_type=MESH,
                 )
@@ -140,17 +144,21 @@
             def _():
                 copy_of(own).start()
 
-            moves.append((sending, own, coming, come, copy_of))
+            moves.append((coming, come, copy_of, way))
+            sent.append((sending, own, copy_of))
         yield
-        for sending, own, coming, come, copy_of in moves:
+        for coming, come, copy_of, way in moves:
             @pl.when(coming)
             def _():
                 copy_of(come).wait_recv()
+
+            if arrived is not None:
+                arrived(step, way, jnp.clip(come, 0, last), coming)
         yield
-        for sending, own, coming, come, copy_of in moves:
-            @pl.when(sending)
-            def _():
-                copy_of(own).wait_send()
+    for sending, own, copy_of in sent:
+        @pl.when(sending)
+        def _():
+            copy_of(own).wait_send()
 
 
 def chain(*lines):
@@ -172,8 +180,7 @@
     me = lax.axis_index("gy")
     z, x = me // x_count, me % x_count
     greet(neighbours(z, x, z_count, x_count))
-    out[z, x] = block[...]
-    left, right = column_parts(block.shape[1])
+    left, right = column_parts(block.shape[1], z_count, x_count)
 
     def along_z(k):
         return k * x_count + x
@@ -181,74 +188,89 @@
     def along_x(k):
         return z * x_count + k
 
+    def pick(ref, *lead):
+        return lambda way, step: ref.at[(*lead, way, step)]
+
+    out[z, x] = block[...]
+
+    def z_first():
+        pending = []
+
+        def onward(k, enabled, slot):
+            line = line_gather(
+                x_count, x, along_x, lambda q: out.at[k, q, :, left],
+                pick(sems[2], slot), pick(sems[3], slot), enabled,
+            )
+            next(line, None)
+            pending.append(line)
+
+        onward(z, None, 0)
+        yield from line_gather(
+            z_count, z, along_z, lambda k: out.at[k, x, :, left], pick(sems[0]), pick(sems[1]),
+            arrived=lambda step, way, k, coming: onward(k, coming, 1 + 2 * step + way),
+        )
+        for line in pending:
+            yield from line
+
     run_together(
+        z_first(),
         chain(
-            line_gather(z_count, z, along_z, lambda k: out.at[k, x, :, left], sems[0], sems[1]),
             line_gather(
-                x_count, x, along_x, lambda k: out.at[:, k, :, left], sems[2], sems[3]
+                x_count, x, along_x, lambda k: out.at[z, k, :, right], pick(sems[4]), pick(sems[5])
+            ),
+            line_gather(
+                z_count, z, along_z, lambda k: out.at[k, :, :, right], pick(sems[6]), pick(sems[7])
             ),
         ),
-        chain(
-            line_gather(x_count, x, along_x, lambda k: out.at[z, k, :, right], sems[4], sems[5]),
-            line_gather(
-                z_count, z, along_z, lambda k: out.at[k, :, :, right], sems[6], sems[7]
-            ),
-        ),
     )
 
 
 def line_reduce(count, pos, device_of, own, store, outgoing, incoming, sends, recvs):
     last = count - 1
-    for step in range(count - 1):
-        moves = []
+
+    def copy_of(way, slot):
+        return pltpu.make_async_remote_copy(
+            src_ref=outgoing.at[way, slot],
+            dst_ref=incoming.at[way, slot],
+            send_sem=sends.at[way, slot],
+            recv_sem=recvs.at[way, slot],
+            device_id={"gy": device_of(jnp.clip(pos + (1 if way == 0 else -1), 0, last))},
+            device_id_type=MESH,
+        )
+
+    behind = (pos, last - pos)
+    for time in range(count - 1):
         for way in (0, 1):
-            toward = 1 if way == 0 else -1
-            dest = last - step if way == 0 else step
-            peer = jnp.clip(pos + toward, 0, last)
-            sending = pos < dest if way == 0 else pos > dest
-            fed = (pos > 0) if way == 0 else (pos < last)
-            coming = fed & ((pos <= dest) if way == 0 else (pos >= dest))
-            copy = pltpu.make_async_remote_copy(
-                src_ref=outgoing.at[way, step],
-                dst_ref=incoming.at[way, step],
-                send_sem=sends.at[way, step],
-                recv_sem=recvs.at[way, step],
-                device_id={"gy": device_of(peer)},
-                device_id_type=MESH,
-            )
-            moves.append((sending, fed, coming, copy, dest, way))
-        for sending, fed, coming, copy, dest, way in moves:
-            @pl.when(coming)
+            slot = jnp.clip(time - behind[way], 0, last - 1)
+            dest = last - slot if way == 0 else slot
+
+            @pl.when((behind[way] > 0) & (behind[way] <= time))
             def _():
-                copy.wait_recv()
-
-            @pl.when(sending & fed)
+                copy_of(way, slot).wait_recv()
+                outgoing[way, slot] = (
+                    own(dest) + incoming[way, slot].astype(jnp.float32)
+                ).astype(jnp.bfloat16)
+                copy_of(way, slot).start()
+
+            @pl.when(behind[way] == 0)
             def _():
-                outgoing[way, step] = (own(dest) + incoming[way, step].astype(jnp.float32)).astype(
-                    jnp.bfloat16
-                )
-
-            @pl.when(sending & jnp.logical_not(fed))
+                outgoing[way, slot] = own(dest).astype(jnp.bfloat16)
+                copy_of(way, slot).start()
+
+        yield
+    store(own(pos))
+    yield
+    for way in (0, 1):
+        @pl.when(behind[way] > 0)
+        def _():
+            slot = jnp.clip(last - behind[way], 0, max(last - 1, 0))
+            copy_of(way, slot).wait_recv()
+            store(None, incoming[way, slot].astype(jnp.float32))
+    for time in range(count - 1):
+        for way in (0, 1):
+            @pl.when(behind[way] <= time)
             def _():
-                outgoing[way, step] = own(dest).astype(jnp.bfloat16)
-
-            @pl.when(sending)
-            def _():
-                copy.start()
-        yield
-        for sending, fed, coming, copy, dest, way in moves:
-            @pl.when(sending)
-            def _():
-                copy.wait_send()
-    store(own(pos))
-    for way in (0, 1):
-        step_of = last - pos if way == 0 else pos
-
-        @pl.when(pos > 0 if way == 0 else pos < last)
-        def _():
-            kept = jnp.clip(step_of, 0, max(last - 1, 0))
-            store(None, incoming[way, kept].astype(jnp.float32))
-    yield
+                copy_of(way, jnp.clip(time - behind[way], 0, last - 1)).wait_send()
 
 
 def reduce_kernel(z_count, x_count, terms, out, sum_l, sum_r, total_l, total_r, *rest):
@@ -256,7 +278,7 @@
     me = lax.axis_index("gy")
     z, x = me // x_count, me % x_count
     greet(neighbours(z, x, z_count, x_count))
-    left, right = column_parts(terms.shape[3])
+    left, right = column_parts(terms.shape[3], z_count, x_count)
 
     def along_z(k):
         return k * x_count + x
@@ -342,15 +364,15 @@
     )
 
 
-def pair(count):
-    sems = pltpu.SemaphoreType.DMA((2, max(count - 1, 1)))
+def pair(count, *lead):
+    sems = pltpu.SemaphoreType.DMA((*lead, 2, max(count - 1, 1)))
     return [sems, sems]
 
 
 def gather_rows(block, identity):
     z_count, x_count = grid_of(lax.axis_size("gy"))
     rows, width = block.shape
-    scratch = pair(z_count) + pair(x_count) + pair(x_count) + pair(z_count)
+    scratch = pair(z_count) + pair(x_count, 2 * z_count - 1) + pair(x_count) + pair(z_count)
     out = call(
         lambda *refs: gather_kernel(z_count, x_count, *refs),
         jax.ShapeDtypeStruct((z_count, x_count, rows, width), jnp.bfloat16),
@@ -363,7 +385,7 @@
     z_count, x_count = grid_of(lax.axis_size("gy"))
     width = terms.shape[1]
     rows = terms.shape[0] // (z_count * x_count)
-    left, right = column_parts(width)
+    left, right = column_parts(width, z_count, x_count)
     l_size, r_size = left.size, right.size
 
     def slots(count, *shape):
@@ -403,14 +425,22 @@
 
 
 def full_weight(weight):
-    rows, width = weight.shape
-    everywhere = lax.all_gather(weight, ("gx", "gy"), axis=0, tiled=False)
+    return lax.all_gather(weight, ("gx", "gy"), axis=0, tiled=False)
+
+
+def full_product(rows, blocks):
     gx_count, gy_count = lax.axis_size("gx"), lax.axis_size("gy")
-    return (
-        everywhere.reshape(gx_count, gy_count, rows, width)
-        .transpose(0, 2, 1, 3)
-        .reshape(gx_count * rows, gy_count * width)
-    )
+    depth, width = blocks.shape[1:]
+    total = jnp.zeros((gy_count, rows.shape[0], width), jnp.float32)
+    for i in range(gx_count):
+        part = rows[:, i * depth : (i + 1) * depth]
+        total = total + jnp.einsum(
+            "jtk,jkn->jtn",
+            jnp.broadcast_to(part[None], (gy_count,) + part.shape),
+            blocks[i * gy_count : (i + 1) * gy_count],
+            preferred_element_type=jnp.float32,
+        )
+    return total.transpose(1, 0, 2).reshape(rows.shape[0], gy_count * width)
 
 
 def weight_columns(weight):
@@ -489,7 +519,7 @@
     own_rows = patch_slots // gy_count
     patches_own = lax.dynamic_slice_in_dim(ordered, gy_index * own_rows, own_rows, 0)
     attended_own = swap_to_rows(attended, 1).reshape(own_rows, full_width)
-    vit_mid = (patches_own.astype(jnp.float32) + dense(attended_own, vit_out)).astype(jnp.bfloat16)
+    vit_mid = (patches_own.astype(jnp.float32) + full_product(attended_own, vit_out)).astype(jnp.bfloat16)
     vit_normed = gather_rows(layer_norm(vit_mid, vit_norm2), 2)
     summed = feed_forward(vit_normed, vit_fc1, vit_fc2, 3)
     vit_final = (vit_mid.astype(jnp.float32) + summed).astype(jnp.bfloat16)
@@ -524,19 +554,22 @@
 
     dec_normed = gather_rows(rms_norm(embedded, dec_norm1), 7)
     dec_triple = dense(dec_normed, dec_qkv).astype(jnp.bfloat16)
-    queries = dec_triple[:, :local_width].reshape(seq_slots, head_count, HEAD_DIM)
     bounds = jnp.cumsum(lengths)
     own_request = request_of(seq_index, bounds)
-    pairs = lax.all_gather(dec_triple[:, local_width:], "gx", axis=0, tiled=True)
-    key_count = pairs.shape[0]
-    pairs = pairs.reshape(key_count, 2, head_count, HEAD_DIM)
+    dec_triple = dec_triple.reshape(seq_slots, 3, local_width)
+    key_rows = lax.all_gather(dec_triple[:, 1], "gx", axis=0, tiled=True)
+    value_rows = lax.all_gather(dec_triple[:, 2], "gx", axis=0, tiled=True)
+    key_count = key_rows.shape[0]
+    key_rows = key_rows.reshape(key_count, head_count, HEAD_DIM)
+    value_rows = value_rows.reshape(key_count, head_count, HEAD_DIM)
     key_index = jnp.arange(key_count, dtype=jnp.int32)
     allowed = (request_of(key_index, bounds)[None, :] == own_request[:, None]) & (
         key_index[None, :] <= seq_index[:, None]
     )
-    dec_attended = local_heads(queries, pairs[:, 0], pairs[:, 1], allowed)
+    queries = dec_triple[:, 0].reshape(seq_slots, head_count, HEAD_DIM)
+    dec_attended = local_heads(queries, key_rows, value_rows, allowed)
     dec_own = swap_to_rows(dec_attended, 8).reshape(seq_rows, full_width)
-    dec_mid = (embedded.astype(jnp.float32) + dense(dec_own, dec_out)).astype(jnp.bfloat16)
+    dec_mid = (embedded.astype(jnp.float32) + full_product(dec_own, dec_out)).astype(jnp.bfloat16)
     mid_normed = gather_rows(rms_norm(dec_mid, dec_norm2), 9)
     summed = feed_forward(mid_normed, dec_fc1, dec_fc2, 10)
     dec_final = (dec_mid.astype(jnp.float32) + summed).astype(jnp.bfloat16)

time: 704 us -> 490 us (0.70)
  Pallas kernels: 535 us -> 301 us
  local copies, waits for them, and re-layouts: 68.2 us -> 35.7 us
  waiting for transfers between devices: 8.29 us -> 40.6 us
  blocking collectives: 11.5 us -> 24.3 us
    pallas_call x3, Pallas kernels: 322 us -> 106 us  [sum_rows(): call(lambda *refs: reduce_kernel(z_count, x_count, *refs), jax.ShapeDtype...]
    reshape x4 -> x2, local copies, waits for them, and re-layouts: 32.1 us -> 0.49 us  [full_product(): return total.transpose(1, 0, 2).reshape(rows.shape[0], gy_count * width)]
    pallas_call x6, Pallas kernels: 169 us -> 141 us  [gather_rows(): call(lambda *refs: gather_kernel(z_count, x_count, *refs), jax.ShapeDtype...]
    all_gather x3 -> x2, waiting for transfers between devices: 0.01 us -> 20.8 us  [full_weight(): return lax.all_gather(weight, ('gx', 'gy'), axis=0, tiled=False)]
    all_gather x0 -> x2, blocking collectives: none -> 16.7 us  [the longest x1 8.57 us: per_device(): value_rows = lax.all_gather(dec_triple[:, 2], 'gx', axis=0, tiled=True)]
    dot_general x0 -> x8, matrix products: none -> 12 us  [full_product(): jnp.einsum('jtk,jkn->jtn', jnp.broadcast_to(part[None], (gy_count,) + par...]
    all_gather x8, waiting for transfers between devices: 2.51 us -> 14.3 us  [weight_columns(): lax.all_gather(weight.reshape(weight.shape[0], -1), 'gx', axis=0, tiled=T...]
    pallas_call x4, Pallas kernels: 43.8 us -> 54.4 us  [swap_to_rows(): call(lambda *refs: swap_kernel(count, *refs), jax.ShapeDtypeStruct((count...]
  transfers between devices with their start and end apart: 11 -> 10, of which waited for: 1 -> 2; matrix products, arithmetic and copies ran while one was open for 16% -> 17% of each run, Pallas kernels for 57% -> 50%
where the time goes in v2:
time: 490 us; the launch traced here: 480 us
  Pallas kernels  301 us (61%)
  matrix products  53.6 us (11%)
  waiting for transfers between devices  40.6 us (8%)
  local copies, waits for them, and re-layouts  35.7 us (7%)
  blocking collectives  24.3 us (5%)
  between operations  15.5 us (3%)
  other arithmetic  9.26 us (2%)
    pallas_call x6, Pallas kernels, gather_rows(): call(lambda *refs: gather_kernel(z_count, x_count, *refs), jax.ShapeDtype...  141 us
    pallas_call x3, Pallas kernels, sum_rows(): call(lambda *refs: reduce_kernel(z_count, x_count, *refs), jax.ShapeDtype...  106 us
    pallas_call x4, Pallas kernels, swap_to_rows(): call(lambda *refs: swap_kernel(count, *refs), jax.ShapeDtypeStruct((count...  54.4 us
    dot_general x2, matrix products, feed_forward(): lax.dot_general(hidden, fc_back, (((1,), (1,)), ((), ())), preferred_elem...  21.5 us
    all_gather x2, waiting for transfers between devices, full_weight(): return lax.all_gather(weight, ('gx', 'gy'), axis=0, tiled=False)  20.8 us
    all_gather x8, waiting for transfers between devices, weight_columns(): lax.all_gather(weight.reshape(weight.shape[0], -1), 'gx', axis=0, tiled=T...  14.3 us
    dot_general x6, matrix products, dense(): return jnp.dot(rows, weight, preferred_element_type=jnp.float32)  12.6 us
    dot_general x8, matrix products, full_product(): jnp.einsum('jtk,jkn->jtn', jnp.broadcast_to(part[None], (gy_count,) + par...  12 us
  transfers between devices with their start and end apart: 10, of which 2 were waited for; matrix products, arithmetic and copies ran while one was open for 17% of the time, Pallas kernels for 50%

profile of v2, /device:TPU:8, one launch (start us, length us, event | category | flops | bytes accessed | tf_op | source)
XLA Modules:
  0.0 480.5 jit_solution(15455390302639186995)
XLA Ops:
  15.4 25.5 %gather_rows.6 = bf16[4,2,96,1408]{3,2,1,0:T(8,128)(2,1)S(1)} custom-call(bf16[96,1408]{1,0:T(8,128)(2,1)S(1)} %copy-done.3), custom_call_target="tpu_custom_call" | custom-call | bytes 60000000 | tf_op jit(solution)/shard_map/gather_rows/pallas_call | solution.py:376
  40.9 2.1 convert_reduce_fusion
  47.1 9.0 %gather_fusion = bf16[512,1408]{1,0:T(8,128)(2,1)S(1)} fusion(bf16[4000,1408]{1,0:T(8,128)(2,1)} %param.27, s32[1024]{0:T(1024)S(1)} %pad_clamp_fusion), kind=kCustom, calls=%fused_computation | custom fusion | bytes 2885632 | tf_op jit(solution)/shard_map/jit(_take)/gather | solution.py:547
  56.4 27.4 %sum_rows.4 = f32[64,1408]{1,0:T(8,128)S(1)} custom-call(bf16[4,2,64,1408]{3,2,1,0:T(8,128)(2,1)S(1)} %select_select_fusion.refs_0_), custom_call_target="tpu_custom_call" | custom-call | bytes 60000000 | tf_op jit(solution)/shard_map/sum_rows/pallas_call | solution.py:408
  84.4 2.2 fusion.9
  86.6 2.1 copy.88
  88.7 2.3 reshape.469
  91.0 3.6 fusion.48
  97.9 12.8 %swap_to_rows.4 = bf16[8,96,176]{2,1,0:T(8,128)(2,1)S(1)} custom-call(bf16[8,96,176]{2,1,0:T(8,128)(2,1)S(1)} %copy.90.refs_0_), custom_call_target="tpu_custom_call" | custom-call | bytes 20000000 | tf_op jit(solution)/shard_map/swap_to_rows/pallas_call | solution.py:419
  111.5 2.1 copy.97
  115.5 2.1 copy.101
  119.6 20.7 %all-gather.33.cloned.1.call-done = bf16[32,352,176]{1,2,0:T(8,128)(2,1)} async-done(((bf16[1,352,176]{1,2,0:T(8,128)(2,1)}), bf16[32,352,176]{1,2,0:T(8,128)(2,1)}) %all-gather.33.cloned.1.call-update) | async-done | bytes 3964944 | tf_op jit(solution)/shard_map/all_gather | solution.py:428
  147.0 26.3 %gather_rows.7 = bf16[4,2,96,1408]{3,2,1,0:T(8,128)(2,1)S(1)} custom-call(bf16[96,1408]{1,0:T(8,128)(2,1)S(1)} %fusion.154.refs_0_), custom_call_target="tpu_custom_call" | custom-call | bytes 60000000 | tf_op jit(solution)/shard_map/gather_rows/pallas_call | solution.py:376
  173.3 14.2 %all-gather.23.cloned.1.call-done = bf16[1408,768]{1,0:T(8,128)(2,1)} async-done(((bf16[352,768]{1,0:T(8,128)(2,1)}), bf16[1408,768]{1,0:T(8,128)(2,1)}) %all-gather.23.cloned.1.call-update) | async-done | bytes 2162704 | tf_op jit(solution)/shard_map/all_gather | solution.py:447
  187.5 12.9 %convolution_convert_fusion = bf16[768,1408]{1,0:T(8,128)(2,1)} fusion(bf16[1408,768]{1,0:T(8,128)(2,1)} %all-gather.23.cloned.1.call-done, bf16[768,1408]{1,0:T(8,128)(2,1)S(1)} %bitcast.114, bf16[1408,768]{1,0:T(8,128)(2,1)} %all-gather.21.cloned.1.call-done), kind=kOutput, calls=%fused_computation.19 | convolution fusion | flops 3361308672 | bytes 8650752 | tf_op jit(solution)/shard_map/dot_general | solution.py:456
  202.1 49.8 %sum_rows.3 = f32[96,1408]{1,0:T(8,128)S(1)} custom-call(bf16[4,2,96,1408]{3,2,1,0:T(8,128)(2,1)S(1)} %bitcast.116), custom_call_target="tpu_custom_call" | custom-call | bytes 60000000 | tf_op jit(solution)/shard_map/sum_rows/pallas_call | solution.py:408
  253.3 33.0 %gather_rows.8 = bf16[4,2,96,1408]{3,2,1,0:T(8,128)(2,1)S(1)} custom-call(bf16[96,1408]{1,0:T(8,128)(2,1)S(1)} %fusion.157.refs_0_), custom_call_target="tpu_custom_call" | custom-call | bytes 60000000 | tf_op jit(solution)/shard_map/gather_rows/pallas_call | solution.py:376
  286.3 2.1 dot_general.78
  288.4 4.2 fusion.30
  292.9 7.6 %all-gather.1 = bf16[768,1,176]{2,0,1:T(8,128)(2,1)S(1)} all-gather(bf16[192,1,176]{2,0,1:T(8,128)(2,1)S(1)} %fusion.176), channel_id=3, replica_groups=mesh['gx'=4,'gy'=8] {'gx'}, dimensions={0}, use_global_device_ids=true | all-gather | bytes 337920 | tf_op jit(solution)/shard_map/all_gather | solution.py:541
  301.2 15.3 %swap_to_rows.5 = bf16[8,64,176]{2,1,0:T(8,128)(2,1)S(1)} custom-call(bf16[8,64,176]{2,1,0:T(8,128)(2,1)S(1)} %bitcast.122), custom_call_target="tpu_custom_call" | custom-call | bytes 20000000 | tf_op jit(solution)/shard_map/swap_to_rows/pallas_call | solution.py:419
  317.3 17.3 %gather_rows.9 = bf16[4,2,64,1408]{3,2,1,0:T(8,128)(2,1)S(1)} custom-call(bf16[64,1408]{1,0:T(8,128)(2,1)S(1)} %fusion.165.refs_0_), custom_call_target="tpu_custom_call" | custom-call | bytes 60000000 | tf_op jit(solution)/shard_map/gather_rows/pallas_call | solution.py:376
  335.7 8.1 %all-gather.3 = bf16[2048,1,176]{0,2,1:T(8,128)(2,1)S(1)} all-gather(bf16[512,1,176]{0,2,1:T(8,128)(2,1)S(1)} %get-tuple-element.17), channel_id=5, replica_groups=mesh['gx'=4,'gy'=8] {'gx'}, dimensions={0}, use_global_device_ids=true | all-gather | bytes 901120 | tf_op jit(solution)/shard_map/all_gather | solution.py:560
  343.8 2.8 fusion
  346.6 8.6 %all-gather.2 = bf16[2048,1,176]{0,2,1:T(8,128)(2,1)S(1)} all-gather(bf16[512,1,176]{0,2,1:T(8,128)(2,1)S(1)} %get-tuple-element.19), channel_id=4, replica_groups=mesh['gx'=4,'gy'=8] {'gx'}, dimensions={0}, use_global_device_ids=true | all-gather | bytes 901120 | tf_op jit(solution)/shard_map/all_gather | solution.py:561
  355.1 2.1 fusion.106
  357.6 13.0 %swap_to_rows.6 = bf16[8,64,176]{2,1,0:T(8,128)(2,1)S(1)} custom-call(bf16[8,64,176]{2,1,0:T(8,128)(2,1)S(1)} %reshape_reshape.7.refs_0_), custom_call_target="tpu_custom_call" | custom-call | bytes 20000000 | tf_op jit(solution)/shard_map/swap_to_rows/pallas_call | solution.py:419
  379.3 18.4 %gather_rows.10 = bf16[4,2,64,1408]{3,2,1,0:T(8,128)(2,1)S(1)} custom-call(bf16[64,1408]{1,0:T(8,128)(2,1)S(1)} %fusion.169.refs_0_), custom_call_target="tpu_custom_call" | custom-call | bytes 60000000 | tf_op jit(solution)/shard_map/gather_rows/pallas_call | solution.py:376
  397.8 8.5 %convolution_convert_fusion.2 = bf16[512,1408]{1,0:T(8,128)(2,1)S(1)} fusion(bf16[1408,768]{1,0:T(8,128)(2,1)} %all-gather.29.cloned.1.call-done, bf16[512,1408]{1,0:T(8,128)(2,1)S(1)} %bitcast.118, bf16[1408,768]{1,0:T(8,128)(2,1)} %all-gather.27.cloned.1.call-done), kind=kOutput, calls=%fused_computation.21 | convolution fusion | flops 2240872448 | bytes 7208960 | tf_op jit(solution)/shard_map/dot_general | solution.py:456
  406.3 28.4 %sum_rows.5 = f32[64,1408]{1,0:T(8,128)S(1)} custom-call(bf16[4,2,64,1408]{3,2,1,0:T(8,128)(2,1)S(1)} %bitcast.119), custom_call_target="tpu_custom_call" | custom-call | bytes 60000000 | tf_op jit(solution)/shard_map/sum_rows/pallas_call | solution.py:408
  435.0 20.7 %gather_rows.11 = bf16[4,2,64,1408]{3,2,1,0:T(8,128)(2,1)S(1)} custom-call(bf16[64,1408]{1,0:T(8,128)(2,1)S(1)} %fusion.162.refs_0_), custom_call_target="tpu_custom_call" | custom-call | bytes 60000000 | tf_op jit(solution)/shard_map/gather_rows/pallas_call | solution.py:376
  457.0 13.4 %swap_to_rows.7 = bf16[8,64,528]{2,1,0:T(8,128)(2,1)S(1)} custom-call(bf16[8,64,528]{2,1,0:T(8,128)(2,1)S(1)} %bitcast.112), custom_call_target="tpu_custom_call" | custom-call | bytes 20000000 | tf_op jit(solution)/shard_map/swap_to_rows/pallas_call | solution.py:419
  (166 shorter events, 46.5 us)
Async XLA Ops:
  6.5 7.2 %copy-start = (s32[8,2]{0,1:T(2,128)S(1)}, s32[8,2]{0,1:T(2,128)}, u32[]{:S(2)}) copy-start(s32[8,2]{0,1:T(2,128)} %param.23) | copy-start | bytes 196
  6.5 4.0 copy-start.9
  6.5 80.1 %all-gather.31.cloned.1.call-start = ((), (), s32[]{:S(2)}) async-start(), calls=%async_computation.5 | async-start | bytes 2027520 | tf_op jit(solution)/shard_map/all_gather | solution.py:447
  7.3 104.2 %all-gather.35.cloned.1.call-start = ((), (), s32[]{:S(2)}) async-start(), calls=%async_computation.7 | async-start | bytes 2027520 | tf_op jit(solution)/shard_map/all_gather | solution.py:447
  8.0 107.5 %all-gather.39.cloned.1.call-start = ((), (), s32[]{:S(2)}) async-start(), calls=%async_computation.9 | async-start | bytes 2027520 | tf_op jit(solution)/shard_map/all_gather | solution.py:447
  8.7 131.6 %all-gather.33.cloned.1.call-start = ((), (), s32[]{:S(2)}) async-start(), calls=%async_computation.6 | async-start | bytes 4460544 | tf_op jit(solution)/shard_map/all_gather | solution.py:428
  8.8 6.6 %copy-start.3 = (bf16[96,1408]{1,0:T(8,128)(2,1)S(1)}, bf16[96,1408]{1,0:T(8,128)(2,1)}, u32[]{:S(2)}) copy-start(bf16[96,1408]{1,0:T(8,128)(2,1)} %refs_0_.1) | copy-start | bytes 811012
  9.3 164.0 %all-gather.21.cloned.1.call-start = ((), (), s32[]{:S(2)}) async-start(), calls=%async_computation | async-start | bytes 2703360 | tf_op jit(solution)/shard_map/all_gather | solution.py:447
  9.9 177.6 %all-gather.23.cloned.1.call-start = ((), (), s32[]{:S(2)}) async-start(), calls=%async_computation.1 | async-start | bytes 2703360 | tf_op jit(solution)/shard_map/all_gather | solution.py:447
  10.5 277.9 %all-gather.25.cloned.1.call-start = ((), (), s32[]{:S(2)}) async-start(), calls=%async_computation.2 | async-start | bytes 2703360 | tf_op jit(solution)/shard_map/all_gather | solution.py:447
  11.6 359.5 %all-gather.37.cloned.1.call-start = ((), (), s32[]{:S(2)}) async-start(), calls=%async_computation.8 | async-start | bytes 4460544 | tf_op jit(solution)/shard_map/all_gather | solution.py:428
  12.4 385.4 %all-gather.27.cloned.1.call-start = ((), (), s32[]{:S(2)}) async-start(), calls=%async_computation.3 | async-start | bytes 2703360 | tf_op jit(solution)/shard_map/all_gather | solution.py:447
  13.1 384.6 %all-gather.29.cloned.1.call-start = ((), (), s32[]{:S(2)}) async-start(), calls=%async_computation.4 | async-start | bytes 2703360 | tf_op jit(solution)/shard_map/all_gather | solution.py:447
  43.0 1.3 copy-start.4
  43.0 2.8 copy-start.10
  43.0 3.1 copy-start.18
  43.0 3.5 copy-start.15
  43.1 3.8 copy-start.16
  88.7 2.3 copy-start.17
  140.4 3.7 copy-start.5
  144.6 2.2 copy-start.11
  200.5 1.6 copy-start.2
  292.9 24.3 %copy-start.13 = (f32[1408]{0:T(1024)S(1)}, f32[1408]{0:T(1024)}, u32[]{:S(2)}) copy-start(f32[1408]{0:T(1024)} %param.36) | copy-start | bytes 16900
  301.2 33.4 %copy-start.7 = (bf16[1408,528]{0,1:T(8,128)(2,1)S(1)}, bf16[1408,528]{0,1:T(8,128)(2,1)}, u32[]{:S(2)}) copy-start(bf16[1408,528]{0,1:T(8,128)(2,1)} %reshape.473) | copy-start | bytes 4460548
  334.6 9.2 %copy-start.8 = (pred[512,2048]{1,0:T(8,128)(4,1)S(1)}, pred[512,2048]{1,0:T(8,128)(4,1)}, u32[]{:S(2)}) copy-start(pred[512,2048]{1,0:T(8,128)(4,1)} %fusion.9) | copy-start | bytes 3145732
  376.6 2.6 copy-start.14
  406.3 28.6 %copy-start.12 = (f32[1408]{0:T(1024)S(1)}, f32[1408]{0:T(1024)}, u32[]{:S(2)}) copy-start(f32[1408]{0:T(1024)} %param.42) | copy-start | bytes 16900
  406.3 49.4 %copy-start.6 = (bf16[1408,528]{0,1:T(8,128)(2,1)S(1)}, bf16[1408,528]{0,1:T(8,128)(2,1)}, u32[]{:S(2)}) copy-start(bf16[1408,528]{0,1:T(8,128)(2,1)} %reshape.477) | copy-start | bytes 4460548
  470.4 2.8 copy-start.1
Sparse Core Ops, SparseCore 0:
  8.9 21.0 all-gather.30
  31.6 19.9 all-gather.34
  53.1 19.9 all-gather.38
  76.0 64.3 all-gather.32
  141.8 21.3 all-gather.20
  164.6 22.9 all-gather.22
  189.1 22.9 all-gather.24
  215.1 68.1 all-gather.36
  284.9 26.3 all-gather.26
  312.7 24.3 all-gather.28

commit v3 on v2

--- a/solution.py
+++ b/solution.py
@@ -491,11 +491,10 @@
     own_grids = lax.dynamic_slice_in_dim(grids, gx_index * per_group, per_group, 0)
     local_width = vit_qkv.shape[2]
     head_count = local_width // HEAD_DIM
-    vit_qkv, vit_fc1, vit_fc2, merge_proj, dec_qkv, dec_fc1, dec_fc2, next_qkv = [
-        weight_columns(weight)
-        for weight in (vit_qkv, vit_fc1, vit_fc2, merge_proj, dec_qkv, dec_fc1, dec_fc2, next_qkv)
+    vit_qkv, vit_fc1, vit_fc2, merge_proj = [
+        weight_columns(weight) for weight in (vit_qkv, vit_fc1, vit_fc2, merge_proj)
     ]
-    vit_out, dec_out = full_weight(vit_out), full_weight(dec_out)
+    vit_out = full_weight(vit_out)
 
     patches_full = gather_rows(patches, 0)
     patch_slots, full_width = patches_full.shape
@@ -516,6 +515,13 @@
         triple[:, 2],
         (image_ids[:, None] == image_ids[None, :]) & is_key[None, :],
     )
+    attended, dec_qkv, dec_out, dec_fc1, dec_fc2 = lax.optimization_barrier(
+        (attended, dec_qkv, dec_out, dec_fc1, dec_fc2)
+    )
+    dec_qkv, dec_fc1, dec_fc2 = [
+        weight_columns(weight) for weight in (dec_qkv, dec_fc1, dec_fc2)
+    ]
+    dec_out = full_weight(dec_out)
     own_rows = patch_slots // gy_count
     patches_own = lax.dynamic_slice_in_dim(ordered, gy_index * own_rows, own_rows, 0)
     attended_own = swap_to_rows(attended, 1).reshape(own_rows, full_width)
@@ -570,6 +576,8 @@
     dec_attended = local_heads(queries, key_rows, value_rows, allowed)
     dec_own = swap_to_rows(dec_attended, 8).reshape(seq_rows, full_width)
     dec_mid = (embedded.astype(jnp.float32) + full_product(dec_own, dec_out)).astype(jnp.bfloat16)
+    dec_mid, next_qkv = lax.optimization_barrier((dec_mid, next_qkv))
+    next_qkv = weight_columns(next_qkv)
     mid_normed = gather_rows(rms_norm(dec_mid, dec_norm2), 9)
     summed = feed_forward(mid_normed, dec_fc1, dec_fc2, 10)
     dec_final = (dec_mid.astype(jnp.float32) + summed).astype(jnp.bfloat16)

time: 490 us -> 496 us (1.012)
    pallas_call x3, Pallas kernels: 106 us -> 111 us  [sum_rows(): call(lambda *refs: reduce_kernel(z_count, x_count, *refs), jax.ShapeDtype...]
  transfers between devices with their start and end apart: 10 -> 10, of which waited for: 2 -> 2; matrix products, arithmetic and copies ran while one was open for 17% -> 16% of each run, Pallas kernels for 50% -> 59%
where the time goes in v3:
time: 496 us; the launch traced here: 488 us
  Pallas kernels  305 us (61%)
  matrix products  54.6 us (11%)
  waiting for transfers between devices  43.8 us (9%)
  local copies, waits for them, and re-layouts  35.1 us (7%)
  blocking collectives  24.2 us (5%)
  between operations  15.2 us (3%)
  other arithmetic  10.1 us (2%)
    pallas_call x6, Pallas kernels, gather_rows(): call(lambda *refs: gather_kernel(z_count, x_count, *refs), jax.ShapeDtype...  138 us
    pallas_call x3, Pallas kernels, sum_rows(): call(lambda *refs: reduce_kernel(z_count, x_count, *refs), jax.ShapeDtype...  111 us
    pallas_call x4, Pallas kernels, swap_to_rows(): call(lambda *refs: swap_kernel(count, *refs), jax.ShapeDtypeStruct((count...  55.1 us
    all_gather x2, waiting for transfers between devices, full_weight(): return lax.all_gather(weight, ('gx', 'gy'), axis=0, tiled=False)  25.5 us
    dot_general x2, matrix products, feed_forward(): lax.dot_general(hidden, fc_back, (((1,), (1,)), ((), ())), preferred_elem...  21.4 us
    all_gather x8, waiting for transfers between devices, weight_columns(): lax.all_gather(weight.reshape(weight.shape[0], -1), 'gx', axis=0, tiled=T...  14.3 us
    dot_general x6, matrix products, dense(): return jnp.dot(rows, weight, preferred_element_type=jnp.float32)  13.6 us
    dot_general x8, matrix products, full_product(): jnp.einsum('jtk,jkn->jtn', jnp.broadcast_to(part[None], (gy_count,) + par...  12 us
  transfers between devices with their start and end apart: 10, of which 2 were waited for; matrix products, arithmetic and copies ran while one was open for 16% of the time, Pallas kernels for 59%

profile of v3, /device:TPU:8, one launch (start us, length us, event | category | flops | bytes accessed | tf_op | source)
XLA Modules:
  0.0 488.3 jit_solution(4457545300614175869)
XLA Ops:
  9.9 25.4 %gather_rows.6 = bf16[4,2,96,1408]{3,2,1,0:T(8,128)(2,1)S(1)} custom-call(bf16[96,1408]{1,0:T(8,128)(2,1)S(1)} %copy-done.3), custom_call_target="tpu_custom_call" | custom-call | bytes 60000000 | tf_op jit(solution)/shard_map/gather_rows/pallas_call | solution.py:376
  36.0 2.1 convert_reduce_fusion
  41.4 2.1 copy.88
  44.7 3.3 fusion.48
  56.3 9.0 %gather_fusion = bf16[512,1408]{1,0:T(8,128)(2,1)S(1)} fusion(bf16[4000,1408]{1,0:T(8,128)(2,1)} %param.27, s32[1024]{0:T(1024)S(1)} %pad_clamp_fusion), kind=kCustom, calls=%fused_computation | custom fusion | bytes 2885632 | tf_op jit(solution)/shard_map/jit(_take)/gather | solution.py:553
  65.6 31.8 %sum_rows.4 = f32[64,1408]{1,0:T(8,128)S(1)} custom-call(bf16[4,2,64,1408]{3,2,1,0:T(8,128)(2,1)S(1)} %select_select_fusion.refs_0_), custom_call_target="tpu_custom_call" | custom-call | bytes 60000000 | tf_op jit(solution)/shard_map/sum_rows/pallas_call | solution.py:408
  98.2 2.2 fusion.9
  100.6 12.8 %swap_to_rows.4 = bf16[8,96,176]{2,1,0:T(8,128)(2,1)S(1)} custom-call(bf16[8,96,176]{2,1,0:T(8,128)(2,1)S(1)} %bitcast.118), custom_call_target="tpu_custom_call" | custom-call | bytes 20000000 | tf_op jit(solution)/shard_map/swap_to_rows/pallas_call | solution.py:419
  114.2 2.1 copy.97
  118.3 25.5 %all-gather.33.cloned.1.call-done = bf16[32,352,176]{1,2,0:T(8,128)(2,1)} async-done(((bf16[1,352,176]{1,2,0:T(8,128)(2,1)}), bf16[32,352,176]{1,2,0:T(8,128)(2,1)}) %all-gather.33.cloned.1.call-update) | async-done | bytes 3964944 | tf_op jit(solution)/shard_map/all_gather | solution.py:428
  150.5 26.2 %gather_rows.7 = bf16[4,2,96,1408]{3,2,1,0:T(8,128)(2,1)S(1)} custom-call(bf16[96,1408]{1,0:T(8,128)(2,1)S(1)} %fusion.154.refs_0_), custom_call_target="tpu_custom_call" | custom-call | bytes 60000000 | tf_op jit(solution)/shard_map/gather_rows/pallas_call | solution.py:376
  176.8 14.2 %all-gather.23.cloned.1.call-done = bf16[1408,768]{1,0:T(8,128)(2,1)} async-done(((bf16[352,768]{1,0:T(8,128)(2,1)}), bf16[1408,768]{1,0:T(8,128)(2,1)}) %all-gather.23.cloned.1.call-update) | async-done | bytes 2162704 | tf_op jit(solution)/shard_map/all_gather | solution.py:447
  191.0 12.9 %convolution_convert_fusion = bf16[768,1408]{1,0:T(8,128)(2,1)} fusion(bf16[1408,768]{1,0:T(8,128)(2,1)} %all-gather.23.cloned.1.call-done, bf16[768,1408]{1,0:T(8,128)(2,1)S(1)} %bitcast.115, bf16[1408,768]{1,0:T(8,128)(2,1)} %all-gather.21.cloned.1.call-done), kind=kOutput, calls=%fused_computation.19 | convolution fusion | flops 3361308672 | bytes 8650752 | tf_op jit(solution)/shard_map/dot_general | solution.py:456
  205.6 50.4 %sum_rows.3 = f32[96,1408]{1,0:T(8,128)S(1)} custom-call(bf16[4,2,96,1408]{3,2,1,0:T(8,128)(2,1)S(1)} %bitcast.116), custom_call_target="tpu_custom_call" | custom-call | bytes 60000000 | tf_op jit(solution)/shard_map/sum_rows/pallas_call | solution.py:408
  257.3 33.1 %gather_rows.8 = bf16[4,2,96,1408]{3,2,1,0:T(8,128)(2,1)S(1)} custom-call(bf16[96,1408]{1,0:T(8,128)(2,1)S(1)} %fusion.157.refs_0_), custom_call_target="tpu_custom_call" | custom-call | bytes 60000000 | tf_op jit(solution)/shard_map/gather_rows/pallas_call | solution.py:376
  290.4 2.1 dot_general.78
  292.6 4.2 fusion.30
  297.1 8.0 %all-gather.1 = bf16[768,1,176]{2,0,1:T(8,128)(2,1)S(1)} all-gather(bf16[192,1,176]{2,0,1:T(8,128)(2,1)S(1)} %fusion.176), channel_id=3, replica_groups=mesh['gx'=4,'gy'=8] {'gx'}, dimensions={0}, use_global_device_ids=true | all-gather | bytes 337920 | tf_op jit(solution)/shard_map/all_gather | solution.py:547
  305.7 14.8 %swap_to_rows.5 = bf16[8,64,176]{2,1,0:T(8,128)(2,1)S(1)} custom-call(bf16[8,64,176]{2,1,0:T(8,128)(2,1)S(1)} %bitcast.123), custom_call_target="tpu_custom_call" | custom-call | bytes 20000000 | tf_op jit(solution)/shard_map/swap_to_rows/pallas_call | solution.py:419
  321.4 18.0 %gather_rows.9 = bf16[4,2,64,1408]{3,2,1,0:T(8,128)(2,1)S(1)} custom-call(bf16[64,1408]{1,0:T(8,128)(2,1)S(1)} %fusion.165.refs_0_), custom_call_target="tpu_custom_call" | custom-call | bytes 60000000 | tf_op jit(solution)/shard_map/gather_rows/pallas_call | solution.py:376
  340.5 7.9 %all-gather.3 = bf16[2048,1,176]{0,2,1:T(8,128)(2,1)S(1)} all-gather(bf16[512,1,176]{0,2,1:T(8,128)(2,1)S(1)} %get-tuple-element.29), channel_id=5, replica_groups=mesh['gx'=4,'gy'=8] {'gx'}, dimensions={0}, use_global_device_ids=true | all-gather | bytes 901120 | tf_op jit(solution)/shard_map/all_gather | solution.py:566
  348.4 8.3 %all-gather.2 = bf16[2048,1,176]{0,2,1:T(8,128)(2,1)S(1)} all-gather(bf16[512,1,176]{0,2,1:T(8,128)(2,1)S(1)} %get-tuple-element.31), channel_id=4, replica_groups=mesh['gx'=4,'gy'=8] {'gx'}, dimensions={0}, use_global_device_ids=true | all-gather | bytes 901120 | tf_op jit(solution)/shard_map/all_gather | solution.py:567
  356.7 2.8 fusion
  359.5 2.1 fusion.106
  362.0 13.0 %swap_to_rows.6 = bf16[8,64,176]{2,1,0:T(8,128)(2,1)S(1)} custom-call(bf16[8,64,176]{2,1,0:T(8,128)(2,1)S(1)} %reshape_reshape.3.refs_0_), custom_call_target="tpu_custom_call" | custom-call | bytes 20000000 | tf_op jit(solution)/shard_map/swap_to_rows/pallas_call | solution.py:419
  383.8 18.0 %gather_rows.10 = bf16[4,2,64,1408]{3,2,1,0:T(8,128)(2,1)S(1)} custom-call(bf16[64,1408]{1,0:T(8,128)(2,1)S(1)} %fusion.169.refs_0_), custom_call_target="tpu_custom_call" | custom-call | bytes 60000000 | tf_op jit(solution)/shard_map/gather_rows/pallas_call | solution.py:376
  401.9 8.5 %convolution_convert_fusion.2 = bf16[512,1408]{1,0:T(8,128)(2,1)S(1)} fusion(bf16[1408,768]{1,0:T(8,128)(2,1)} %all-gather.29.cloned.1.call-done, bf16[512,1408]{1,0:T(8,128)(2,1)S(1)} %bitcast.119, bf16[1408,768]{1,0:T(8,128)(2,1)} %all-gather.27.cloned.1.call-done), kind=kOutput, calls=%fused_computation.21 | convolution fusion | flops 2240872448 | bytes 7208960 | tf_op jit(solution)/shard_map/dot_general | solution.py:456
  410.4 28.9 %sum_rows.5 = f32[64,1408]{1,0:T(8,128)S(1)} custom-call(bf16[4,2,64,1408]{3,2,1,0:T(8,128)(2,1)S(1)} %bitcast.121), custom_call_target="tpu_custom_call" | custom-call | bytes 60000000 | tf_op jit(solution)/shard_map/sum_rows/pallas_call | solution.py:408
  439.6 17.6 %gather_rows.11 = bf16[4,2,64,1408]{3,2,1,0:T(8,128)(2,1)S(1)} custom-call(bf16[64,1408]{1,0:T(8,128)(2,1)S(1)} %fusion.162.refs_0_), custom_call_target="tpu_custom_call" | custom-call | bytes 60000000 | tf_op jit(solution)/shard_map/gather_rows/pallas_call | solution.py:376
  457.2 2.1 copy.101
  461.3 2.4 convolution_convert_fusion.3
  464.0 14.5 %swap_to_rows.7 = bf16[8,64,528]{2,1,0:T(8,128)(2,1)S(1)} custom-call(bf16[8,64,528]{2,1,0:T(8,128)(2,1)S(1)} %bitcast.112), custom_call_target="tpu_custom_call" | custom-call | bytes 20000000 | tf_op jit(solution)/shard_map/swap_to_rows/pallas_call | solution.py:419
  (166 shorter events, 46.8 us)
Async XLA Ops:
  6.5 0.8 copy-start
  6.5 34.9 %all-gather.31.cloned.1.call-start = ((), (), s32[]{:S(2)}) async-start(), calls=%async_computation.5 | async-start | bytes 2027520 | tf_op jit(solution)/shard_map/all_gather | solution.py:447
  7.3 107.0 %all-gather.35.cloned.1.call-start = ((), (), s32[]{:S(2)}) async-start(), calls=%async_computation.7 | async-start | bytes 2027520 | tf_op jit(solution)/shard_map/all_gather | solution.py:447
  8.9 1.0 copy-start.3
  38.1 1.3 copy-start.4
  43.5 1.2 copy-start.17
  44.7 3.3 copy-start.8
  49.4 3.3 copy-start.9
  50.6 5.2 %copy-start.10 = (f32[4,1408]{1,0:T(4,128)S(1)}, f32[4,1408]{1,0:T(4,128)}, u32[]{:S(2)}) copy-start(f32[4,1408]{1,0:T(4,128)} %param.34) | copy-start | bytes 67588
  50.7 93.2 %all-gather.33.cloned.1.call-start = ((), (), s32[]{:S(2)}) async-start(), calls=%async_computation.6 | async-start | bytes 4460544 | tf_op jit(solution)/shard_map/all_gather | solution.py:428
  51.4 125.4 %all-gather.21.cloned.1.call-start = ((), (), s32[]{:S(2)}) async-start(), calls=%async_computation | async-start | bytes 2703360 | tf_op jit(solution)/shard_map/all_gather | solution.py:447
  52.0 4.1 copy-start.16
  52.0 139.0 %all-gather.23.cloned.1.call-start = ((), (), s32[]{:S(2)}) async-start(), calls=%async_computation.1 | async-start | bytes 2703360 | tf_op jit(solution)/shard_map/all_gather | solution.py:447
  52.6 240.0 %all-gather.25.cloned.1.call-start = ((), (), s32[]{:S(2)}) async-start(), calls=%async_computation.2 | async-start | bytes 2703360 | tf_op jit(solution)/shard_map/all_gather | solution.py:447
  53.7 321.9 %all-gather.37.cloned.1.call-start = ((), (), s32[]{:S(2)}) async-start(), calls=%async_computation.8 | async-start | bytes 4460544 | tf_op jit(solution)/shard_map/all_gather | solution.py:428
  54.5 347.4 %all-gather.27.cloned.1.call-start = ((), (), s32[]{:S(2)}) async-start(), calls=%async_computation.3 | async-start | bytes 2703360 | tf_op jit(solution)/shard_map/all_gather | solution.py:447
  55.2 346.6 %all-gather.29.cloned.1.call-start = ((), (), s32[]{:S(2)}) async-start(), calls=%async_computation.4 | async-start | bytes 2703360 | tf_op jit(solution)/shard_map/all_gather | solution.py:447
  65.3 32.2 %copy-start.18 = (s32[8]{0:T(128)S(1)}, s32[8]{0:T(128)}, u32[]{:S(2)}) copy-start(s32[8]{0:T(128)} %param.26) | copy-start | bytes 100
  65.3 32.4 %copy-start.15 = (s32[768]{0:T(1024)S(1)}, s32[768]{0:T(1024)}, u32[]{:S(2)}) copy-start(s32[768]{0:T(1024)} %param.25) | copy-start | bytes 9220
  114.2 343.0 %all-gather.39.cloned.1.call-start = ((), (), s32[]{:S(2)}) async-start(), calls=%async_computation.9 | async-start | bytes 2027520 | tf_op jit(solution)/shard_map/all_gather | solution.py:447
  143.8 3.7 copy-start.5
  148.1 2.2 copy-start.11
  203.9 1.6 copy-start.2
  297.1 24.2 %copy-start.13 = (f32[1408]{0:T(1024)S(1)}, f32[1408]{0:T(1024)}, u32[]{:S(2)}) copy-start(f32[1408]{0:T(1024)} %param.36) | copy-start | bytes 16900
  305.7 33.7 %copy-start.6 = (bf16[1408,528]{0,1:T(8,128)(2,1)S(1)}, bf16[1408,528]{0,1:T(8,128)(2,1)}, u32[]{:S(2)}) copy-start(bf16[1408,528]{0,1:T(8,128)(2,1)} %reshape.481) | copy-start | bytes 4460548
  340.5 16.3 %copy-start.7 = (pred[512,2048]{1,0:T(8,128)(4,1)S(1)}, pred[512,2048]{1,0:T(8,128)(4,1)}, u32[]{:S(2)}) copy-start(pred[512,2048]{1,0:T(8,128)(4,1)} %fusion.9) | copy-start | bytes 3145732
  381.0 2.6 copy-start.14
  410.4 29.1 %copy-start.12 = (f32[1408]{0:T(1024)S(1)}, f32[1408]{0:T(1024)}, u32[]{:S(2)}) copy-start(f32[1408]{0:T(1024)} %param.42) | copy-start | bytes 16900
  478.5 2.8 copy-start.1
Sparse Core Ops, SparseCore 0:
  8.9 21.0 all-gather.30
  50.8 23.8 all-gather.34
  77.7 66.0 all-gather.32
  145.2 21.3 all-gather.20
  168.0 22.9 all-gather.22
  192.4 22.9 all-gather.24
  218.4 68.8 all-gather.36
  288.9 25.4 all-gather.26
  316.0 23.9 all-gather.28
  401.9 22.5 all-gather.38
